TPU v7x, 128 devices: a whole 4x4x4 slice. The times are simulated.
128 devices in a mesh: pool: 16 (over x, y), tp: 8 (over z, core).
Axes of the slice: x: 4, y: 4, z: 4, core: 2. Of those that a mesh axis runs over, the one named last changes fastest.
Arguments:
- tokens: bfloat16 [3072, 8192], P('pool', 'tp'), may hold values from -6 to 6
- w_query: bfloat16 [8192, 8192], P(None, 'tp'), may hold values from -0.0625 to 0.0625
- w_key: bfloat16 [8192, 1024], P(None, 'tp'), may hold values from -0.0625 to 0.0625
- w_value: bfloat16 [8192, 1024], P(None, 'tp'), may hold values from -0.0625 to 0.0625
- kv_pool: bfloat16 [1024, 8, 2, 64, 128], P('pool', 'tp'), may hold values from -42 to 42
- page_owner: int32 [48, 128, 1], P('pool'), may hold values from 0 to 15; in each aligned block of 384 rows (0 to 383, 384 to 767, ..., all dimensions but the last counted through in order) at most 32 rows name the same one
- page_slot: int32 [48, 128], P('pool'), may hold values from 0 to 63
- prefix_len: int32 [48], P('pool'), may hold values from 2048 to 8192, as said below
Outputs:
- attended: bfloat16 [3072, 8192], P('pool', 'tp')
- suffix_kv: bfloat16 [3072, 2, 8, 128], P('pool', None, 'tp')
Inputs may be any that keep to these rules, and one draw needn't show every extreme that they name: `page_owner`: within the rows of one index of pool (3 x 128 entries) no owner appears more than 32 times, and some owner appears exactly 32 times. `prefix_len`: some node has exactly 8192 prefix tokens and another exactly 2048.
All inputs are finite; a program needn't handle non-finite values.
Results may differ from a plain program's by a relative error of at most 0.0065.
The roundings to bfloat16 on the way count: a program that leaves them out, or rounds other values in their place, can miss the bound.
Values may be sent and summed in bfloat16 or wider, within the bound.
No kernel may reach another device: no remote copies, remote signals or barrier semaphores. Data moves between devices by JAX's collectives and lax.ppermute only.
A program may use at most 192 MiB of HBM per device.

v0:
```python
import jax
import jax.numpy as jnp
from jax import lax
from jax.sharding import PartitionSpec as P

QH = 64
KVH = 8
HD = 128
SUF = 64
MAXP = 128


rope_base = 500000.0
norm_eps = 1e-05


def rotate(values, positions):
    half_dim = values.shape[-1] // 2
    inverse = rope_base ** (-(jnp.arange(half_dim, dtype=jnp.float32) * 2.0 / values.shape[-1]))
    angles = positions[..., None] * inverse
    cosine = jnp.cos(angles)
    sine_part = jnp.sin(angles)
    first_half = values[..., :half_dim]
    second_half = values[..., half_dim:]
    return jnp.concatenate(
        [
            first_half * cosine - second_half * sine_part,
            second_half * cosine + first_half * sine_part,
        ],
        axis=-1,
    )


def attend_node(queries, keys_new, values_new, node_pages, length):
    suffix_len, kv_heads, group_size, head_dim = queries.shape
    pages_count, page_len = (node_pages.shape[0], node_pages.shape[3])
    score_scale = head_dim ** (-0.5)
    prefix_keys = node_pages[:, :, 0]
    prefix_vals = node_pages[:, :, 1]
    prefix_scores = jnp.einsum(
        "skgd,pkjd->kgspj", queries, prefix_keys, preferred_element_type=jnp.float32
    )
    prefix_scores = (
        prefix_scores.reshape(kv_heads, group_size, suffix_len, pages_count * page_len)
        * score_scale
    )
    key_place = jnp.arange(pages_count * page_len, dtype=jnp.int32)
    prefix_scores = jnp.where(key_place < length, prefix_scores, -jnp.inf)
    own_scores = (
        jnp.einsum("skgd,tkd->kgst", queries, keys_new, preferred_element_type=jnp.float32)
        * score_scale
    )
    causal = jnp.arange(suffix_len)[:, None] >= jnp.arange(suffix_len)[None, :]
    own_scores = jnp.where(causal, own_scores, -jnp.inf)
    peak = jnp.maximum(prefix_scores.max(-1), own_scores.max(-1))
    prefix_weights = jnp.exp(prefix_scores - peak[..., None])
    own_weights = jnp.exp(own_scores - peak[..., None])
    weight_sum = prefix_weights.sum(-1) + own_weights.sum(-1)
    prefix_round = prefix_weights.astype(jnp.bfloat16).reshape(
        kv_heads, group_size, suffix_len, pages_count, page_len
    )
    own_round = own_weights.astype(jnp.bfloat16)
    combined = jnp.einsum(
        "kgspj,pkjd->kgsd", prefix_round, prefix_vals, preferred_element_type=jnp.float32
    )
    combined = combined + jnp.einsum(
        "kgst,tkd->kgsd", own_round, values_new, preferred_element_type=jnp.float32
    )
    combined = combined / weight_sum[..., None]
    return (
        jnp.transpose(combined, (2, 0, 1, 3))
        .reshape(suffix_len, kv_heads * group_size * head_dim)
        .astype(jnp.bfloat16)
    )


def body(tokens, w_query, w_key, w_value, kv_pool, page_owner, page_slot, prefix_len):
    gathered = lax.all_gather(tokens, "tp", axis=1, tiled=True)
    widened = gathered.astype(jnp.float32)
    normed = (
        widened * lax.rsqrt(jnp.mean(widened * widened, axis=-1, keepdims=True) + norm_eps)
    ).astype(jnp.bfloat16)
    node_count = prefix_len.shape[0]
    local_heads = w_query.shape[1] // HD
    local_kv = w_key.shape[1] // HD
    queries = jnp.dot(normed, w_query, preferred_element_type=jnp.float32).reshape(
        node_count, SUF, local_heads, HD
    )
    keys_new = jnp.dot(normed, w_key, preferred_element_type=jnp.float32).reshape(
        node_count, SUF, local_kv, HD
    )
    values_new = jnp.dot(normed, w_value, preferred_element_type=jnp.float32).reshape(
        node_count, SUF, local_kv, HD
    )
    positions = (prefix_len[:, None] + jnp.arange(SUF, dtype=jnp.int32)[None, :]).astype(
        jnp.float32
    )[:, :, None]
    queries = rotate(queries, positions).astype(jnp.bfloat16)
    keys_new = rotate(keys_new, positions).astype(jnp.bfloat16)
    values_new = values_new.astype(jnp.bfloat16)
    suffix_kv = jnp.stack([keys_new, values_new], axis=2).reshape(node_count * SUF, 2, local_kv, HD)
    owners = page_owner[..., 0].reshape(-1)
    slot_ids = page_slot.reshape(-1)
    slot_count = kv_pool.shape[0]
    pool_all = lax.all_gather(kv_pool, "pool", axis=0, tiled=True)
    fetched = pool_all[owners * slot_count + slot_ids]
    node_pages = fetched.reshape((node_count, MAXP) + kv_pool.shape[1:])

    def one_node(node_items):
        node_query, node_keys, node_values, node_table, node_length = node_items
        return attend_node(
            node_query.reshape(SUF, local_kv, QH // KVH, HD),
            node_keys,
            node_values,
            node_table,
            node_length,
        )

    attended = lax.map(one_node, (queries, keys_new, values_new, node_pages, prefix_len))
    return (attended.reshape(node_count * SUF, local_heads * HD), suffix_kv)


def solution(mesh):
    in_specs = (
        P("pool", "tp"),
        P(None, "tp"),
        P(None, "tp"),
        P(None, "tp"),
        P("pool", "tp", None, None, None),
        P("pool", None, None),
        P("pool", None),
        P("pool"),
    )
    out_specs = (P("pool", "tp"), P("pool", None, "tp", None))
    return jax.shard_map(body, mesh=mesh, in_specs=in_specs, out_specs=out_specs, check_vma=False)
```

profile of v0, /device:TPU:1, one launch (start us, length us, event | category | flops | bytes accessed | tf_op | source)
XLA Modules:
  0.0 338.0 jit_solution(232870043459519112)
XLA Ops:
  7.2 0.7 all-gather.5.cloned.1.call-update
  7.9 0.0 all-gather.3.cloned.1.call-start
  8.0 0.7 all-gather.3.cloned.1.call-update
  8.7 0.7 fusion.44
  9.4 0.7 add_convert_fusion.1
  10.2 0.4 multiply_cosine_fusion.1
  10.6 30.8 %all-gather.5.cloned.1.call-done = bf16[192,8192]{1,0:T(8,128)(2,1)} async-done(((bf16[192,1024]{1,0:T(8,128)(2,1)}), bf16[192,8192]{1,0:T(8,128)(2,1)}) %all-gather.5.cloned.1.call-update) | async-done | bytes 3145744 | tf_op jit(solution)/shard_map/all_gather | solution.py:78
  41.3 2.6 fusion.34
  44.0 8.7 %convolution_bitcast_fusion = f32[24,8,8,128]{3,1,2,0:T(8,128)S(1)} fusion(bf16[8192,1024]{1,0:T(8,128)(2,1)} %param.11, bf16[192,8192]{1,0:T(8,128)(2,1)} %all-gather.5.cloned.1.call-done, f32[192]{0:T(256)S(1)} %add_rsqrt_fusion), kind=kOutput, calls=%fused_computation.48 | convolution fusion | flops 3225944064 | bytes 20710144 | tf_op jit(solution)/shard_map/dot_general | solution.py:86
  52.7 0.1 copy.44
  52.8 1.1 fusion.46
  53.9 0.5 fusion.41
  54.4 0.3 copy-done.5
  54.7 1.1 convolution_convert_fusion
  55.7 0.1 pad_maximum_fusion.1
  55.8 0.7 copy.36
  56.6 0.1 pad_maximum_fusion.2
  56.7 0.3 fusion.50
  56.9 0.3 subtract_convert_fusion
  57.3 0.2 pad_maximum_fusion
  57.5 182.4 %all-gather.3.cloned.1.call-done = bf16[1024,1,2,64,128]{4,3,2,1,0:T(8,128)(2,1)} async-done(((bf16[64,1,2,64,128]{4,3,2,1,0:T(8,128)(2,1)}), bf16[1024,1,2,64,128]{4,3,2,1,0:T(8,128)(2,1)}) %all-gather.3.cloned.1.call-update) | async-done | bytes 33554448 | tf_op jit(solution)/shard_map/all_gather | solution.py:105
  239.9 11.9 %gather_fusion = bf16[384,2,64,128]{3,2,1,0:T(8,128)(2,1)} fusion(bf16[1024,2,64,128]{3,2,1,0:T(8,128)(2,1)} %bitcast.166, s32[1024]{0:T(1024)S(1)} %pad_clamp_fusion), kind=kCustom, calls=%fused_computation | custom fusion | bytes 25167360 | tf_op jit(solution)/shard_map/gather | solution.py:106
  251.8 77.6 %while.10 = (s32[]{:T(128)}, bf16[3,64,1024]{2,1,0:T(8,128)(2,1)S(1)}, s32[3]{0:T(128)S(1)}, bf16[3,128,1,2,64,128]{5,4,3,1,0,2:T(8,128)(2,1)}, bf16[3,64,8,128]...) while((s32[]{:T(128)}, ...), condition=%wide.region_6.7_spmd, body=%wide.region_1.6_spmd.sunk | while | flops 2210851840 | bytes 140756112 | solution.py:119
  251.8 3.1 constant_dynamic-slice_fusion.2
  255.0 2.7 copy.54
  257.7 0.7 dynamic_slice.53
  258.3 0.6 add_compare_fusion.2
  259.0 2.7 bitcast_reduce_fusion.2
  261.7 0.3 fusion.65
  261.9 3.2 fusion.66
  265.2 2.2 copy-done.2
  267.4 9.8 %fusion.67 = f32[8,64]{1,0:T(8,128)S(1)} fusion(f32[128,64,64,8]{0,2,3,1:T(8,128)} %copy-done.2, f32[8,64]{1,0:T(8,128)S(1)} %max.10, pred[128,64]{0,1:T(8,128)(4,1)S(1)} %add_compare_fusion.2), kind=kLoop, calls=%fused_computation.5.clone.1 | loop fusion | flops 16776704 | bytes 16789504 | tf_op jit(solution)/shard_map/while/body/eval_jaxpr/reduce_sum | solution.py:58
  277.2 0.1 fusion.68
  277.2 0.2 fusion.69
  277.5 0.1 copy.55
  277.6 0.1 convert_element_type.119
  277.7 3.2 constant_dynamic-slice_fusion.2
  280.8 2.7 copy.54
  283.5 0.7 dynamic_slice.53
  284.2 0.6 add_compare_fusion.2
  284.8 2.7 bitcast_reduce_fusion.2
  287.5 0.3 fusion.65
  287.8 3.2 fusion.66
  291.1 2.2 copy-done.2
  293.2 9.8 %fusion.67 = f32[8,64]{1,0:T(8,128)S(1)} fusion(f32[128,64,64,8]{0,2,3,1:T(8,128)} %copy-done.2, f32[8,64]{1,0:T(8,128)S(1)} %max.10, pred[128,64]{0,1:T(8,128)(4,1)S(1)} %add_compare_fusion.2), kind=kLoop, calls=%fused_computation.5.clone.1 | loop fusion | flops 16776704 | bytes 16789504 | tf_op jit(solution)/shard_map/while/body/eval_jaxpr/reduce_sum | solution.py:58
  303.0 0.1 fusion.68
  303.1 0.2 fusion.69
  303.3 0.1 copy.55
  303.4 0.1 convert_element_type.119
  303.5 3.2 constant_dynamic-slice_fusion.2
  306.7 2.7 copy.54
  309.4 0.7 dynamic_slice.53
  310.1 0.6 add_compare_fusion.2
  310.7 2.7 bitcast_reduce_fusion.2
  313.4 0.3 fusion.65
  313.7 3.2 fusion.66
  316.9 2.2 copy-done.2
  319.1 9.8 %fusion.67 = f32[8,64]{1,0:T(8,128)S(1)} fusion(f32[128,64,64,8]{0,2,3,1:T(8,128)} %copy-done.2, f32[8,64]{1,0:T(8,128)S(1)} %max.10, pred[128,64]{0,1:T(8,128)(4,1)S(1)} %add_compare_fusion.2), kind=kLoop, calls=%fused_computation.5.clone.1 | loop fusion | flops 16776704 | bytes 16789504 | tf_op jit(solution)/shard_map/while/body/eval_jaxpr/reduce_sum | solution.py:58
  328.9 0.1 fusion.68
  329.0 0.2 fusion.69
  329.2 0.1 copy.55
  329.3 0.1 convert_element_type.119
  329.4 0.7 copy-done.6
  330.2 1.0 copy-done.1
  (29 shorter events, 0.2 us)
Async XLA Ops:
  7.2 45.7 %copy-start = (bf16[8192,128]{1,0:T(8,128)(2,1)S(1)}, bf16[8192,128]{1,0:T(8,128)(2,1)}, u32[]{:S(2)}) copy-start(bf16[8192,128]{1,0:T(8,128)(2,1)} %param.12) | copy-start | bytes 6291460
  7.2 34.2 %all-gather.5.cloned.1.call-start = ((), (), s32[]{:S(2)}) async-start(), calls=%async_computation.1 | async-start | bytes 3538944 | tf_op jit(solution)/shard_map/all_gather | solution.py:78
  7.9 232.0 %all-gather.3.cloned.1.call-start = ((), (), s32[]{:S(2)}) async-start(), calls=%async_computation | async-start | bytes 35651584 | tf_op jit(solution)/shard_map/all_gather | solution.py:105
  44.0 8.9 %copy-start.3 = (bf16[192,8192]{1,0:T(8,128)(2,1)S(1)}, bf16[192,8192]{1,0:T(8,128)(2,1)}, u32[]{:S(2)}) copy-start(bf16[192,8192]{1,0:T(8,128)(2,1)} %all-gather.5.cloned.1.call-done) | copy-start | bytes 9437188
  52.7 2.0 copy-start.5
  239.9 11.9 %copy-start.4 = (s32[3]{0:T(128)S(1)}, s32[3]{0:T(128)}, u32[]{:S(2)}) copy-start(s32[3]{0:T(128)} %param.17) | copy-start | bytes 40
  261.6 5.7 %copy-start.2 = (f32[128,64,64,8]{0,2,3,1:T(8,128)}, f32[128,64,64,8]{0,2,3,1:T(8,128)S(1)}, u32[]{:S(2)}) copy-start(f32[128,64,64,8]{0,2,3,1:T(8,128)S(1)} %get-tuple-element.140) | copy-start | bytes 50331652 | tf_op jit(solution)/shard_map/while
  287.5 5.7 %copy-start.2 = (f32[128,64,64,8]{0,2,3,1:T(8,128)}, f32[128,64,64,8]{0,2,3,1:T(8,128)S(1)}, u32[]{:S(2)}) copy-start(f32[128,64,64,8]{0,2,3,1:T(8,128)S(1)} %get-tuple-element.140) | copy-start | bytes 50331652 | tf_op jit(solution)/shard_map/while
  313.4 5.7 %copy-start.2 = (f32[128,64,64,8]{0,2,3,1:T(8,128)}, f32[128,64,64,8]{0,2,3,1:T(8,128)S(1)}, u32[]{:S(2)}) copy-start(f32[128,64,64,8]{0,2,3,1:T(8,128)S(1)} %get-tuple-element.140) | copy-start | bytes 50331652 | tf_op jit(solution)/shard_map/while
  329.4 0.7 copy-start.6
  329.4 1.7 copy-start.1
Sparse Core Ops, SparseCore 0:
  9.7 31.5 all-gather.4
  43.5 196.3 all-gather.2
where the time goes:
time: 339 us; the launch traced here: 338 us
  waiting for transfers between devices  215 us (63%)
  local copies, waits for them, and re-layouts  41.6 us (12%)
  other arithmetic  37.2 us (11%)
  matrix products  30 us (9%)
  between operations  14.2 us (4%)
    all_gather x1, waiting for transfers between devices, body(): pool_all = lax.all_gather(kv_pool, 'pool', axis=0, tiled=True)  182 us
    all_gather x1, waiting for transfers between devices, body(): gathered = lax.all_gather(tokens, 'tp', axis=1, tiled=True)  30.8 us
    reduce_sum x6, other arithmetic, attend_node(): weight_sum = prefix_weights.sum(-1) + own_weights.sum(-1)  29.6 us
    dynamic_slice x9, local copies, waits for them, and re-layouts, body(): lax.map(one_node, (queries, keys_new, values_new, node_pages, prefix_len))  19.5 us
    gather x1, local copies, waits for them, and re-layouts, body(): fetched = pool_all[owners * slot_count + slot_ids]  11.9 us
    dot_general x3, matrix products, attend_node(): jnp.einsum('kgspj,pkjd->kgsd', prefix_round, prefix_vals, preferred_eleme...  9.73 us
    dot_general x1, matrix products, body(): jnp.dot(normed, w_query, preferred_element_type=jnp.float32)  8.68 us
    dot_general x3, matrix products, attend_node(): jnp.einsum('skgd,pkjd->kgspj', queries, prefix_keys, preferred_element_ty...  7.98 us
  transfers between devices with their start and end apart: 2, of which 2 were waited for; matrix products, arithmetic and copies ran while one was open for 5% of the time, Pallas kernels for 0%

commit v1 on v0

v1 whole, which is shorter than its diff:
```python
import functools
import math

import jax
import jax.numpy as jnp
from jax import lax
from jax.experimental import pallas as pl
from jax.experimental.pallas import tpu as pltpu
from jax.sharding import PartitionSpec as P

HD = 128
SUF = 64
PAGE = 64
MAXP = 128
NODES = 3
GROUPS = 4
HEADS = 8
ROWS = HEADS * SUF
BLOCK = 8
KEYS = BLOCK * PAGE
FEATURES = 8192

rope_base = 500000.0
norm_eps = 1e-05
FACTOR = math.log2(math.e) / math.sqrt(HD)
LOW = -1e30

AX = ("pool", "tp")
EVERY = [(x, y, z, c) for x in range(4) for y in range(4) for z in range(4) for c in range(2)]


def flat(x, y, z, c):
    return ((x % 4) * 4 + y % 4) * 8 + (z % 4) * 2 + c


def page_shift(s):
    return [(flat(x, y, z, c), flat(x + s * c, y + s * (1 - c), z, c)) for x, y, z, c in EVERY]


def query_shift(s):
    return [(flat(x, y, z, c), flat(x + s * (1 - c), y + s * c, z, c)) for x, y, z, c in EVERY]


def z_shift(s):
    return [(flat(x, y, z, c), flat(x, y, z + s, c)) for x, y, z, c in EVERY]


def core_swap():
    return [(flat(x, y, z, c), flat(x, y, z, 1 - c)) for x, y, z, c in EVERY]


def project_kernel(shape, ranks, *refs):
    refs = list(refs)
    groups = [[refs.pop(0) for _ in range(n)] for n in shape]
    wq, wk, wv, cos, sin, q_out, kv_out, w_s, x_s, sems = refs

    copies = []
    for t in range(4):
        copies.append([pltpu.make_async_copy(wq.at[:, pl.ds(t * 256, 256)], w_s.at[t], sems.at[t])])
    copies.append(
        [
            pltpu.make_async_copy(wk, w_s.at[4, :, pl.ds(0, 128)], sems.at[4]),
            pltpu.make_async_copy(wv, w_s.at[4, :, pl.ds(128, 128)], sems.at[5]),
        ]
    )
    for some in copies:
        for copy in some:
            copy.start()
    load = lambda group: jnp.concatenate([r[...] for r in group], axis=0) if len(group) > 1 else group[0][...]
    total = jnp.zeros((192, 128), jnp.float32)
    for group in groups:
        wide = load(group).astype(jnp.float32)
        for k in range(8):
            part = wide[:, k * 128 : (k + 1) * 128]
            total = total + part * part
    scale = lax.rsqrt(jnp.sum(total, axis=-1, keepdims=True) * (1.0 / FEATURES) + norm_eps)
    for i, group in enumerate(groups):
        x_s[ranks[i]] = (load(group).astype(jnp.float32) * scale).astype(jnp.bfloat16)
    for t, some in enumerate(copies):
        for copy in some:
            copy.wait()
        total = None
        for r in range(8):
            part = jnp.dot(x_s[r], w_s[t, r * 1024 : (r + 1) * 1024, :], preferred_element_type=jnp.float32)
            total = part if total is None else total + part
        for h in range(2):
            u = total[:, h * HD : (h + 1) * HD]
            g = t * 2 + h
            if g <= HEADS:
                u = u * cos[...] + pltpu.roll(u, 64, 1) * sin[...]
            u = u.astype(jnp.bfloat16)
            if g < HEADS:
                q_out[:, g * HD : (g + 1) * HD] = u
            else:
                kv_out[:, (g - HEADS) * HD : (g - HEADS + 1) * HD] = u


def project(xs, ranks, wq, wk, wv, rope):
    shape = tuple(len(g) for g in xs)
    flat_xs = [a for g in xs for a in g]
    vmem = pl.BlockSpec(memory_space=pltpu.VMEM)
    hbm = pl.BlockSpec(memory_space=pltpu.HBM)
    outs = [jax.ShapeDtypeStruct((192, 1024), jnp.bfloat16), jax.ShapeDtypeStruct((192, 256), jnp.bfloat16)]
    return pl.pallas_call(
        functools.partial(project_kernel, shape),
        out_shape=outs,
        in_specs=[pl.BlockSpec(memory_space=pltpu.SMEM)] + [vmem] * len(flat_xs) + [hbm] * 3 + [vmem] * 2,
        out_specs=[vmem] * 2,
        scratch_shapes=[
            pltpu.VMEM((5, FEATURES, 256), jnp.bfloat16),
            pltpu.VMEM((8, 192, 1024), jnp.bfloat16),
            pltpu.SemaphoreType.DMA((6,)),
        ],
        compiler_params=pltpu.CompilerParams(vmem_limit_bytes=48 * 2**20),
        cost_estimate=pl.CostEstimate(flops=10**6, bytes_accessed=10**6, transcendentals=0),
    )(jnp.stack(ranks).astype(jnp.int32), *flat_xs, wq, wk, wv, *rope)


def attend_kernel(groups, plan, idx, steps, keys, *refs):
    refs = list(refs)
    take = lambda n: [refs.pop(0) for _ in range(n)]
    pages = take(len(plan))
    qs = take(len(groups))
    own = groups == (3,)
    suffix = take(1)[0] if own else None
    outs = [take(2 if own else 1) for _ in groups]
    pool, q_s, s_s, mx_s, acc_s, sems = refs

    copies = []
    for i, (at, ref) in enumerate(zip(plan, pages)):
        copies.append(pltpu.make_async_copy(ref.at[:, 0], pool.at[pl.ds(at, ref.shape[0])], sems.at[i]))
    for copy in copies:
        copy.start()
    for k, q in enumerate(qs):
        for n in range(NODES):
            for g in range(HEADS):
                q_s[k * NODES + n, g * SUF : (g + 1) * SUF, :] = q[n * SUF : (n + 1) * SUF, g * HD : (g + 1) * HD]
    for copy in copies:
        copy.wait()

    lane = lax.broadcasted_iota(jnp.int32, (1, KEYS), 1)
    ones = jnp.ones((KEYS, HD), jnp.bfloat16)

    def node(n, _):
        row = n + groups[0] * NODES
        mx_s[...] = jnp.full_like(mx_s, LOW)
        limit = keys[row]

        def scores(i, _):
            k = jnp.concatenate([pool[idx[row, i * BLOCK + u], 0] for u in range(BLOCK)], axis=0)
            s = lax.dot_general(q_s[n], k, (((1,), (1,)), ((), ())), preferred_element_type=jnp.float32)
            s = s + jnp.where(lane + i * KEYS < limit, 0.0, LOW)
            s_s[i] = s
            top = mx_s[...]
            for u in range(KEYS // 128):
                top = jnp.maximum(top, s[:, u * 128 : (u + 1) * 128])
            mx_s[...] = top
            return 0

        lax.fori_loop(0, steps[row], scores, 0)
        peak = jnp.max(mx_s[...], axis=-1, keepdims=True)
        if own:
            local = n
            r = pl.ds(pl.multiple_of(local * SUF, SUF), SUF)
            s_new = lax.dot_general(q_s[n], suffix[r, :HD], (((1,), (1,)), ((), ())), preferred_element_type=jnp.float32)
            i = lax.broadcasted_iota(jnp.int32, (ROWS, SUF), 0) % SUF
            j = lax.broadcasted_iota(jnp.int32, (ROWS, SUF), 1)
            s_new = jnp.where(j <= i, s_new, LOW)
            peak = jnp.maximum(jnp.max(s_new, axis=-1, keepdims=True), peak)
        shift = peak * FACTOR
        if own:
            w = jnp.exp2(s_new * FACTOR - shift).astype(jnp.bfloat16)
            v = jnp.concatenate([suffix[r, HD:], ones[:SUF]], axis=1)
            acc_s[...] = jnp.dot(w, v, preferred_element_type=jnp.float32)
        else:
            acc_s[...] = jnp.zeros_like(acc_s)

        def values(i, _):
            v = jnp.concatenate([pool[idx[row, i * BLOCK + u], 1] for u in range(BLOCK)], axis=0)
            w = jnp.exp2(s_s[i] * FACTOR - shift).astype(jnp.bfloat16)
            acc_s[...] += jnp.dot(w, jnp.concatenate([v, ones], axis=1), preferred_element_type=jnp.float32)
            return 0

        lax.fori_loop(0, steps[row], values, 0)

        at = lax.broadcasted_iota(jnp.int32, (SUF, 128), 1)
        total = jnp.ones((SUF, 128), jnp.float32)
        level = jnp.full((SUF, 128), LOW, jnp.float32)
        for g in range(HEADS):
            rows = slice(g * SUF, (g + 1) * SUF)
            total = jnp.where(at == g, acc_s[rows, HD:], total)
            level = jnp.where(at == g, shift[rows], level)
        some = total > 0.0
        total = jnp.where(some, total, 1.0)
        level = jnp.where(some, level + jnp.log2(total), LOW)
        share = jnp.where(some, 1.0 / total, 0.0)
        if not own:
            tile = jnp.where(at < HEADS, level, 0.0)
            high = tile.astype(jnp.bfloat16).astype(jnp.float32)
            rest = tile - high
            mid = rest.astype(jnp.bfloat16).astype(jnp.float32)
            level = high + pltpu.roll(mid, 8, 1) + pltpu.roll(rest - mid, 16, 1)

        def put(out, local):
            r = pl.ds(pl.multiple_of(local * SUF, SUF), SUF)
            for g in range(HEADS):
                o = acc_s[g * SUF : (g + 1) * SUF, :HD] * share[:, g : g + 1]
                out[0][r, g * HD : (g + 1) * HD] = o.astype(out[0].dtype)
            if own:
                out[1][r, :] = level
            else:
                out[0][r, HEADS * HD :] = level.astype(jnp.bfloat16)

        for k in range(len(groups)):

            @pl.when((n >= k * NODES) & (n < (k + 1) * NODES))
            def _():
                put(outs[k], n - k * NODES)

        return 0

    lax.fori_loop(0, len(groups) * NODES, node, 0)


def attend(groups, lists, pages, qs, suffix):
    own = groups == (3,)
    f32 = jnp.float32
    if own:
        outs = [jax.ShapeDtypeStruct((192, 1024), f32), jax.ShapeDtypeStruct((192, 128), f32)]
    else:
        outs = [jax.ShapeDtypeStruct((192, 1152), jnp.bfloat16) for _ in groups]
    n = len(groups) * NODES
    extra = [suffix] if own else []
    vmem = pl.BlockSpec(memory_space=pltpu.VMEM)
    smem = pl.BlockSpec(memory_space=pltpu.SMEM)
    hbm = pl.BlockSpec(memory_space=pl.ANY)
    return pl.pallas_call(
        functools.partial(attend_kernel, groups, tuple(at for at, _ in pages)),
        out_shape=outs,
        in_specs=[smem] * 3 + [hbm] * len(pages) + [vmem] * (len(qs) + len(extra)),
        out_specs=[vmem] * len(outs),
        scratch_shapes=[
            pltpu.VMEM((sum(a.shape[0] for _, a in pages), 2, PAGE, HD), jnp.bfloat16),
            pltpu.VMEM((n, ROWS, HD), jnp.bfloat16),
            pltpu.VMEM((MAXP // BLOCK, ROWS, KEYS), f32),
            pltpu.VMEM((ROWS, 128), f32),
            pltpu.VMEM((ROWS, 2 * HD), f32),
            pltpu.SemaphoreType.DMA((len(pages),)),
        ],
        compiler_params=pltpu.CompilerParams(vmem_limit_bytes=36 * 2**20),
        cost_estimate=pl.CostEstimate(flops=10**9, bytes_accessed=10**6, transcendentals=0),
    )(*lists, *[a for _, a in pages], *qs, *extra)


def merge_kernel(o_ref, l_ref, a_ref, b_ref, c_ref, out_ref):
    others = [a_ref, b_ref, c_ref]
    levels = [l_ref[...]]
    for r in others:
        t = r[:, HEADS * HD :].astype(jnp.float32)
        levels.append(t + pltpu.roll(t, 120, 1) + pltpu.roll(t, 112, 1))
    top = functools.reduce(jnp.maximum, levels)
    weights = [jnp.exp2(v - top) for v in levels]
    share = 1.0 / functools.reduce(jnp.add, weights)
    weights = [w * share for w in weights]
    for g in range(HEADS):
        cols = slice(g * HD, (g + 1) * HD)
        out = o_ref[:, cols] * weights[0][:, g : g + 1]
        for w, r in zip(weights[1:], others):
            out = out + r[:, cols].astype(jnp.float32) * w[:, g : g + 1]
        out_ref[:, cols] = out.astype(jnp.bfloat16)


def make_lists(mask, where, lens):
    place = jnp.arange(MAXP, dtype=jnp.int32)
    upto = jnp.sum(jnp.where(place[None, None, :] <= place[None, :, None], mask[:, None, :], False).astype(jnp.int32), axis=-1)
    hit = mask[:, None, :] & (upto[:, None, :] - 1 == place[None, :, None])
    idx = jnp.sum(jnp.where(hit, where[:, None, :], 0), axis=-1)
    count = jnp.sum(mask.astype(jnp.int32), axis=-1)
    keys = jnp.sum(jnp.where(mask, jnp.minimum(PAGE, lens[:, None] - place[None, :] * PAGE), 0), axis=-1)
    return idx, (count + BLOCK - 1) // BLOCK, keys


def body(tokens, w_query, w_key, w_value, kv_pool, page_owner, page_slot, prefix_len):
    pool_at, tp_at = lax.axis_index("pool"), lax.axis_index("tp")
    x, y, core = pool_at // 4, pool_at % 4, tp_at % 2
    along_page = jnp.where(core == 0, y, x)
    along_query = jnp.where(core == 0, x, y)
    move = lambda a, perm: lax.ppermute(a, AX, perm)

    tok_a, tok_b = move(tokens, z_shift(1)), move(tokens, z_shift(-1))
    tok_o = move(tokens, core_swap())
    page_a, page_b = move(kv_pool, page_shift(1)), move(kv_pool, page_shift(-1))
    positions = (prefix_len[:, None] + jnp.arange(SUF, dtype=jnp.int32)[None, :]).astype(jnp.float32).reshape(192, 1)
    inverse = rope_base ** (-(jnp.arange(HD // 2, dtype=jnp.float32) * 2.0 / HD))
    angles = positions * inverse
    cosine, sine = jnp.cos(angles), jnp.sin(angles)
    rope = (jnp.concatenate([cosine, cosine], axis=1), jnp.concatenate([-sine, sine], axis=1))

    tok_ao, tok_bo = move(tok_a, core_swap()), move(tok_b, core_swap())
    tok_c, tok_d = move(tok_a[:96], z_shift(1)), move(tok_b[96:], z_shift(-1))
    tok_co, tok_do = move(tok_c, core_swap()), move(tok_d, core_swap())

    table = jnp.concatenate(
        [page_owner[..., 0] * 64 + page_slot, jnp.broadcast_to(jnp.pad(prefix_len, (0, MAXP - NODES))[None], (1, MAXP))], axis=0
    )
    table = lax.optimization_barrier((table, tok_a, tok_b))[0]
    tables = [move(table, query_shift(-1)), move(table, query_shift(1)), move(table, query_shift(2)), table]

    page_a, page_b, tok_co, tok_do = lax.optimization_barrier((page_a, page_b, tok_co, tok_do))
    page_c, page_d = move(page_a[:32], page_shift(1)), move(page_b[32:], page_shift(-1))
    z = tp_at // 2
    rank = lambda dz, same: ((z + dz) % 4) * 2 + (core if same else 1 - core)
    blocks = [[tokens], [tok_o], [tok_a], [tok_b], [tok_ao], [tok_bo], [tok_c, tok_d], [tok_co, tok_do]]
    ranks = [rank(dz, same) for dz, same in ((0, 1), (0, 0), (-1, 1), (1, 1), (-1, 0), (1, 0), (2, 1), (2, 0))]
    queries, suffix = project(blocks, ranks, w_query, w_key, w_value, rope)
    suffix_kv = suffix.reshape(192, 2, 1, HD)

    qs = [move(queries, query_shift(-1)), move(queries, query_shift(1)), move(queries, query_shift(2))]

    pages = ((0, kv_pool), (64, page_a), (128, page_b), (192, page_c), (224, page_d))
    codes = jnp.concatenate([t[:NODES] for t in tables], axis=0)
    lens = jnp.concatenate([t[NODES, :NODES] for t in tables], axis=0)
    owner, slot = codes // 64, codes % 64
    owner_page = jnp.where(core == 0, owner % 4, owner // 4)
    owner_query = jnp.where(core == 0, owner // 4, owner % 4)
    apart = (owner_page - along_page) % 4
    needed = (owner_query == along_query) & (jnp.arange(MAXP, dtype=jnp.int32)[None, :] * PAGE < lens[:, None])
    start = jnp.where(apart == 0, 0, jnp.where(apart == 3, 64, jnp.where(apart == 1, 128, 192)))
    lists = make_lists(needed, start + slot, lens)
    sent = attend((0, 1, 2), lists, pages, qs, None)
    back = [move(r, query_shift(s)) for r, s in zip(sent, (1, -1, 2))]
    mine = attend((3,), lists, pages, [queries], suffix)
    attended = pl.pallas_call(
        merge_kernel,
        out_shape=jax.ShapeDtypeStruct((192, 1024), jnp.bfloat16),
        compiler_params=pltpu.CompilerParams(vmem_limit_bytes=16 * 2**20),
    )(*mine, *back)
    return attended, suffix_kv


def solution(mesh):
    in_specs = (
        P("pool", "tp"),
        P(None, "tp"),
        P(None, "tp"),
        P(None, "tp"),
        P("pool", "tp", None, None, None),
        P("pool", None, None),
        P("pool", None),
        P("pool"),
    )
    out_specs = (P("pool", "tp"), P("pool", None, "tp", None))
    return jax.shard_map(body, mesh=mesh, in_specs=in_specs, out_specs=out_specs, check_vma=False)
```

time: 339 us -> 118 us (0.35)
  waiting for transfers between devices: 215 us -> 16.8 us
  Pallas kernels: 0 us -> 53.2 us
  other arithmetic: 37.2 us -> 3.47 us
  starting transfers between devices: 0.08 us -> 33.2 us
  local copies, waits for them, and re-layouts: 41.6 us -> 9.5 us
  matrix products: 30 us -> 0 us
  between operations: 14.2 us -> 0.9 us
    all_gather x2 -> x0, waiting for transfers between devices: 213 us -> none  [the longest x1 182 us: body(): pool_all = lax.all_gather(kv_pool, 'pool', axis=0, tiled=True)]
    pallas_call x0 -> x4, Pallas kernels: none -> 53.2 us  [the longest x2 38 us: attend(): pl.pallas_call(functools.partial(attend_kernel, groups, tuple((at for at,...]
    ppermute x0 -> x22, starting transfers between devices: none -> 33.2 us  [body(): move = lambda a, perm: lax.ppermute(a, AX, perm)]
    reduce_sum x7 -> x3, other arithmetic: 32.2 us -> 0.77 us  [the longest x1 0.31 us: make_lists(): idx = jnp.sum(jnp.where(hit, where[:, None, :], 0), axis=-1)]
    dot_general x15 -> x0, matrix products: 30 us -> none  [the longest x3 9.73 us: attend_node(): jnp.einsum('kgspj,pkjd->kgsd', prefix_round, prefix_vals, preferred_eleme...]
    dynamic_slice x9 -> x0, local copies, waits for them, and re-layouts: 19.5 us -> none  [body(): lax.map(one_node, (queries, keys_new, values_new, node_pages, prefix_len))]
    ppermute x0 -> x22, waiting for transfers between devices: none -> 16.8 us  [body(): move = lambda a, perm: lax.ppermute(a, AX, perm)]
    gather x1 -> x0, local copies, waits for them, and re-layouts: 11.9 us -> none  [body(): fetched = pool_all[owners * slot_count + slot_ids]]
  transfers between devices with their start and end apart: 2 -> 22, of which waited for: 2 -> 7; matrix products, arithmetic and copies ran while one was open for 5% -> 7% of each run, Pallas kernels for 0% -> 21%
where the time goes in v1:
time: 118 us; the launch traced here: 117 us
  Pallas kernels  53.2 us (45%)
  starting transfers between devices  33.2 us (28%)
  waiting for transfers between devices  16.8 us (14%)
  local copies, waits for them, and re-layouts  9.5 us (8%)
  other arithmetic  3.47 us (3%)
    pallas_call x2, Pallas kernels, attend(): pl.pallas_call(functools.partial(attend_kernel, groups, tuple((at for at,...  38 us
    ppermute x22, starting transfers between devices, body(): move = lambda a, perm: lax.ppermute(a, AX, perm)  33.2 us
    ppermute x22, waiting for transfers between devices, body(): move = lambda a, perm: lax.ppermute(a, AX, perm)  16.8 us
    pallas_call x1, Pallas kernels, project(): pl.pallas_call(functools.partial(project_kernel, shape), out_shape=outs,...  12.1 us
    unnamed x22, local copies, waits for them, and re-layouts  4.73 us
    pallas_call x1, Pallas kernels, body(): pl.pallas_call(merge_kernel, out_shape=jax.ShapeDtypeStruct((192, 1024),...  3.13 us
  transfers between devices with their start and end apart: 22, of which 7 were waited for; matrix products, arithmetic and copies ran while one was open for 7% of the time, Pallas kernels for 21%

profile of v1, /device:TPU:1, one launch (start us, length us, event | category | flops | bytes accessed | tf_op | source)
XLA Modules:
  0.0 117.1 jit_solution(12552137726108532970)
XLA Ops:
  0.6 4.7 %collective-permute-start.1 = (bf16[192,1024]{1,0:T(8,128)(2,1)}, bf16[192,1024]{1,0:T(8,128)(2,1)S(1)}, u32[]{:S(2)}, u32[]{:S(2)}) collective-permute-start(bf16[192,1024]{1,0:T(8,128)(2,1)} %refs_0_.3), channel_id=1, source_target_pairs={{0,6},{1,7},{2,0},{3,1},{4,2},{5,3},{6,4},{7,5},{8,14},{9,15},{10,... | collective-permute-start | bytes 1179656 | tf_op jit(solution)/shard_map/ppermute | solution.py:288
  5.3 0.0 collective-permute-start
  5.3 1.2 %collective-permute-start.5 = (bf16[64,1,2,64,128]{4,3,2,1,0:T(8,128)(2,1)}, bf16[64,1,2,64,128]{4,3,2,1,0:T(8,128)(2,1)S(1)}, u32[]{:S(2)}, u32[]{:S(2)}) collective-permute-start(bf16[64,1,2,64,128]{4,3,2,1,0:T(8,128)(2,1)} %refs_0_.5), channel_id=1, source_target_pairs={{0,8},{1,33},{2,10},{3,35},{4,12},{5,37},{6,14},{7,39},{8,16},{9,4... | collective-permute-start | bytes 6291464 | tf_op jit(solution)/shard_map/ppermute | solution.py:288
  6.5 1.5 %collective-permute-start.6 = (bf16[64,1,2,64,128]{4,3,2,1,0:T(8,128)(2,1)}, bf16[64,1,2,64,128]{4,3,2,1,0:T(8,128)(2,1)}, u32[]{:S(2)}, u32[]{:S(2)}) collective-permute-start(bf16[64,1,2,64,128]{4,3,2,1,0:T(8,128)(2,1)} %refs_0_.5), channel_id=1, source_target_pairs={{0,24},{1,97},{2,26},{3,99},{4,28},{5,101},{6,30},{7,103},{8,0},{9... | collective-permute-start | bytes 6291464 | tf_op jit(solution)/shard_map/ppermute | solution.py:288
  8.0 0.7 pad_bitcast_fusion
  8.6 0.7 bitcast_add_fusion
  9.3 0.6 iota_compare_fusion.1
  10.0 0.7 add_convert_fusion
  10.7 0.1 convert_element_type.19
  10.8 0.1 stack.35.ranks
  10.9 0.4 fusion.1
  11.3 0.1 pad_maximum_fusion
  11.4 2.0 %collective-permute-done.1.refs_3_ = bf16[192,1024]{1,0:T(8,128)(2,1)S(1)} collective-permute-done((bf16[192,1024]{1,0:T(8,128)(2,1)}, bf16[192,1024]{1,0:T(8,128)(2,1)S(1)}, u32[]{:S(2)}, u32[]{:S(2)}) %collective-permute-start.1) | collective-permute-done | bytes 393248 | tf_op jit(solution)/shard_map/ppermute | solution.py:288
  13.4 3.1 %collective-permute-done.refs_2_ = bf16[192,1024]{1,0:T(8,128)(2,1)} collective-permute-done((bf16[192,1024]{1,0:T(8,128)(2,1)}, bf16[192,1024]{1,0:T(8,128)(2,1)}, u32[]{:S(2)}, u32[]{:S(2)}) %collective-permute-start) | collective-permute-done | bytes 393248 | tf_op jit(solution)/shard_map/ppermute | solution.py:288
  16.5 2.9 %collective-permute-start.4 = (s32[4,128]{1,0:T(4,128)S(1)}, s32[4,128]{1,0:T(4,128)S(1)}, u32[]{:S(2)}, u32[]{:S(2)}) collective-permute-start(s32[4,128]{1,0:T(4,128)S(1)} %pad_add_fusion.1), channel_id=1, source_target_pairs={{0,64},{1,17},{2,66},{3,19},{4,68},{5,21},{6,70},{7,23},{8,72},{9,... | collective-permute-start | bytes 6152 | tf_op jit(solution)/shard_map/ppermute | solution.py:288
  19.4 0.4 collective-permute-start.3
  19.8 2.3 %collective-permute-start.2 = (s32[4,128]{1,0:T(4,128)S(1)}, s32[4,128]{1,0:T(4,128)S(1)}, u32[]{:S(2)}, u32[]{:S(2)}) collective-permute-start(s32[4,128]{1,0:T(4,128)S(1)} %pad_add_fusion.1), channel_id=1, source_target_pairs={{0,96},{1,25},{2,98},{3,27},{4,100},{5,29},{6,102},{7,31},{8,104},... | collective-permute-start | bytes 6152 | tf_op jit(solution)/shard_map/ppermute | solution.py:288
  22.1 0.9 slice.48
  23.0 0.0 collective-permute-done.4
  23.0 0.3 collective-permute-start.9
  23.3 0.1 collective-permute-done.3
  23.4 1.2 collective-permute-start.7
  24.6 0.0 collective-permute-done.2
  24.6 3.1 %collective-permute-start.13 = (bf16[192,1024]{1,0:T(8,128)(2,1)}, bf16[192,1024]{1,0:T(8,128)(2,1)S(1)}, u32[]{:S(2)}, u32[]{:S(2)}) collective-permute-start(bf16[192,1024]{1,0:T(8,128)(2,1)} %refs_0_.3), channel_id=1, source_target_pairs={{0,1},{1,0},{2,3},{3,2},{4,5},{5,4},{6,7},{7,6},{8,9},{9,8},{10,11... | collective-permute-start | bytes 1179656 | tf_op jit(solution)/shard_map/ppermute | solution.py:288
  27.7 0.3 collective-permute-done.9.refs_7_
  28.0 3.3 %collective-permute-start.10 = (bf16[96,1024]{1,0:T(8,128)(2,1)S(1)}, bf16[96,1024]{1,0:T(8,128)(2,1)S(1)}, u32[]{:S(2)}, u32[]{:S(2)}) collective-permute-start(bf16[96,1024]{1,0:T(8,128)(2,1)S(1)} %collective-permute-done.9.refs_7_), channel_id=1, source_target_pairs={{0,1},{1,0},{2,3},{3,2},{4,5},{5,4},{6,7},{7,6},{8,9},{9,8},{10,11... | collective-permute-start | bytes 589832 | tf_op jit(solution)/shard_map/ppermute | solution.py:288
  31.3 0.0 collective-permute-done.7.refs_6_
  31.3 1.8 %collective-permute-start.8 = (bf16[96,1024]{1,0:T(8,128)(2,1)S(1)}, bf16[96,1024]{1,0:T(8,128)(2,1)S(1)}, u32[]{:S(2)}, u32[]{:S(2)}) collective-permute-start(bf16[96,1024]{1,0:T(8,128)(2,1)S(1)} %collective-permute-done.7.refs_6_), channel_id=1, source_target_pairs={{0,1},{1,0},{2,3},{3,2},{4,5},{5,4},{6,7},{7,6},{8,9},{9,8},{10,11... | collective-permute-start | bytes 589832 | tf_op jit(solution)/shard_map/ppermute | solution.py:288
  33.1 0.0 collective-permute-done.10.refs_9_
  33.2 0.1 collective-permute-start.14
  33.3 0.9 collective-permute-done.8.refs_8_
  34.2 0.4 collective-permute-start.15
  34.6 0.0 collective-permute-done.5.refs_1_
  34.6 0.1 slice.46
  34.7 0.1 collective-permute-start.11
  34.8 1.3 %slice.47 = bf16[32,1,2,64,128]{4,3,2,1,0:T(8,128)(2,1)S(1)} slice(bf16[64,1,2,64,128]{4,3,2,1,0:T(8,128)(2,1)} %collective-permute-done.6.refs_2_), slice={[32:64], [0:1], [0:2], [0:64], [0:128]} | slice | bytes 2097152 | tf_op jit(solution)/shard_map/slice | solution.py:310
  36.1 2.9 %collective-permute-start.12 = (bf16[32,1,2,64,128]{4,3,2,1,0:T(8,128)(2,1)S(1)}, bf16[32,1,2,64,128]{4,3,2,1,0:T(8,128)(2,1)S(1)}, u32[]{:S(2)}, u32[]{:S(2)}) collective-permute-start(bf16[32,1,2,64,128]{4,3,2,1,0:T(8,128)(2,1)S(1)} %slice.47), channel_id=1, source_target_pairs={{0,24},{1,97},{2,26},{3,99},{4,28},{5,101},{6,30},{7,103},{8,0},{9... | collective-permute-start | bytes 3145736 | tf_op jit(solution)/shard_map/ppermute | solution.py:288
  39.0 0.1 pad_add_fusion.2
  39.1 0.2 select_reduce_fusion.1
  39.3 0.3 convert_reduce_fusion
  39.5 0.0 collective-permute-done.13.refs_1_
  39.6 0.0 collective-permute-done.14.refs_4_
  39.6 0.0 copy-start
  39.6 12.1 %shard_map.95 = (bf16[192,1024]{1,0:T(8,128)(2,1)S(1)}, bf16[192,256]{1,0:T(8,128)(2,1)S(1)}) custom-call(s32[8]{0:T(128)S(1)} %stack.35.ranks, bf16[192,1024]{1,0:T(8,128)(2,1)S(1)} %copy-done.7, bf16[192,1024]{1,0:T(8,128)(2,1)S(1)} %collective-permute-done.13.refs_1_, bf16[192,1024]{1,0:T(8,128)(2,1)} %collective-permute-done.refs_2_, ...), custom_call_target="tpu_custom_call" | custom-call | flops 1000000 | bytes 1000000 | tf_op jit(solution)/shard_map/pallas_call | solution.py:104
  51.7 0.0 copy-start.8
  51.7 2.8 %collective-permute-start.16 = (bf16[192,1024]{1,0:T(8,128)(2,1)S(1)}, bf16[192,1024]{1,0:T(8,128)(2,1)S(1)}, u32[]{:S(2)}, u32[]{:S(2)}) collective-permute-start(bf16[192,1024]{1,0:T(8,128)(2,1)S(1)} %get-tuple-element.19.refs_5_), channel_id=1, source_target_pairs={{0,96},{1,25},{2,98},{3,27},{4,100},{5,29},{6,102},{7,31},{8,104},... | collective-permute-start | bytes 1179656 | tf_op jit(solution)/shard_map/ppermute | solution.py:288
  54.5 1.6 %collective-permute-start.18 = (bf16[192,1024]{1,0:T(8,128)(2,1)S(1)}, bf16[192,1024]{1,0:T(8,128)(2,1)S(1)}, u32[]{:S(2)}, u32[]{:S(2)}) collective-permute-start(bf16[192,1024]{1,0:T(8,128)(2,1)S(1)} %get-tuple-element.19.refs_5_), channel_id=1, source_target_pairs={{0,64},{1,17},{2,66},{3,19},{4,68},{5,21},{6,70},{7,23},{8,72},{9,... | collective-permute-start | bytes 1179656 | tf_op jit(solution)/shard_map/ppermute | solution.py:288
  56.2 0.3 select_reduce_fusion.idx
  56.5 7.0 %collective-permute-done.16.refs_5_ = bf16[192,1024]{1,0:T(8,128)(2,1)S(1)} collective-permute-done((bf16[192,1024]{1,0:T(8,128)(2,1)S(1)}, bf16[192,1024]{1,0:T(8,128)(2,1)S(1)}, u32[]{:S(2)}, u32[]{:S(2)}) %collective-permute-start.16) | collective-permute-done | bytes 393248 | tf_op jit(solution)/shard_map/ppermute | solution.py:288
  63.5 3.4 %collective-permute-done.17.refs_6_ = bf16[192,1024]{1,0:T(8,128)(2,1)S(1)} collective-permute-done((bf16[192,1024]{1,0:T(8,128)(2,1)S(1)}, bf16[192,1024]{1,0:T(8,128)(2,1)S(1)}, u32[]{:S(2)}, u32[]{:S(2)}) %collective-permute-start.17) | collective-permute-done | bytes 393248 | tf_op jit(solution)/shard_map/ppermute | solution.py:288
  66.9 0.0 collective-permute-done.12.refs_4_
  66.9 25.9 %shard_map.97 = (bf16[192,1152]{1,0:T(8,128)(2,1)}, bf16[192,1152]{1,0:T(8,128)(2,1)}, bf16[192,1152]{1,0:T(8,128)(2,1)}) custom-call(s32[12,128]{1,0:T(8,128)S(1)} %select_reduce_fusion.idx, s32[12]{0:T(128)S(1)} %and_select_fusion.steps, s32[12]{0:T(128)S(1)} %get-tuple-element.30.keys, bf16[64,1,2,64,128]{4,3,2,1,0:T(8,128)(2,1)S(1)} %copy-done, ...), custom_call_target="tpu_custom_call" | custom-call | flops 1000000000 | bytes 1000000 | tf_op jit(solution)/shard_map/pallas_call | solution.py:237
  92.8 0.1 collective-permute-start.19
  92.9 2.7 %collective-permute-start.20 = (bf16[192,1152]{1,0:T(8,128)(2,1)}, bf16[192,1152]{1,0:T(8,128)(2,1)}, u32[]{:S(2)}, u32[]{:S(2)}) collective-permute-start(bf16[192,1152]{1,0:T(8,128)(2,1)} %get-tuple-element.24), channel_id=1, source_target_pairs={{0,96},{1,25},{2,98},{3,27},{4,100},{5,29},{6,102},{7,31},{8,104},... | collective-permute-start | bytes 1327112 | tf_op jit(solution)/shard_map/ppermute | solution.py:288
  95.5 0.0 collective-permute-start.21
  95.5 1.6 %reshape.379 = bf16[192,2,1,128]{3,1,0,2:T(2,128)(2,1)} reshape(bf16[192,256]{1,0:T(8,128)(2,1)} %copy-done.5) | data formatting | bytes 196608 | tf_op jit(solution)/shard_map/reshape | solution.py:316
  97.1 1.6 %copy-done.1 = bf16[64,1,2,64,128]{4,3,2,1,0:T(8,128)(2,1)S(1)} copy-done((bf16[64,1,2,64,128]{4,3,2,1,0:T(8,128)(2,1)S(1)}, bf16[64,1,2,64,128]{4,3,2,1,0:T(8,128)(2,1)}, u32[]{:S(2)}) %copy-start.1) | copy-done | bytes 2097176
  98.7 1.2 %copy-done.3 = bf16[32,1,2,64,128]{4,3,2,1,0:T(8,128)(2,1)S(1)} copy-done((bf16[32,1,2,64,128]{4,3,2,1,0:T(8,128)(2,1)S(1)}, bf16[32,1,2,64,128]{4,3,2,1,0:T(8,128)(2,1)}, u32[]{:S(2)}) %copy-start.3) | copy-done | bytes 1048600
  99.9 0.9 copy-done.6
  100.8 1.0 copy-done.9
  101.8 12.1 %shard_map.96 = (f32[192,1024]{1,0:T(8,128)S(1)}, f32[192,128]{1,0:T(8,128)S(1)}) custom-call(s32[12,128]{1,0:T(8,128)S(1)} %select_reduce_fusion.idx, s32[12]{0:T(128)S(1)} %and_select_fusion.steps, s32[12]{0:T(128)S(1)} %get-tuple-element.30.keys, bf16[64,1,2,64,128]{4,3,2,1,0:T(8,128)(2,1)S(1)} %copy-done.1, ...), custom_call_target="tpu_custom_call" | custom-call | flops 1000000000 | bytes 1000000 | tf_op jit(solution)/shard_map/pallas_call | solution.py:237
  113.9 0.0 collective-permute-done.19.a_ref
  114.0 0.0 collective-permute-done.20.b_ref
  114.0 3.1 %shard_map.98 = bf16[192,1024]{1,0:T(8,128)(2,1)} custom-call(f32[192,1024]{1,0:T(8,128)S(1)} %get-tuple-element.21.o_ref, f32[192,128]{1,0:T(8,128)S(1)} %get-tuple-element.22.l_ref, bf16[192,1152]{1,0:T(8,128)(2,1)} %collective-permute-done.19.a_ref, bf16[192,1152]{1,0:T(8,128)(2,1)} %collective-permute-done.20.b_ref, ...), custom_call_target="tpu_custom_call" | custom-call | tf_op jit(solution)/shard_map/pallas_call | solution.py:333
  (32 shorter events, 0.1 us)
Async XLA Ops:
  0.6 12.8 %collective-permute-start.1 = (bf16[192,1024]{1,0:T(8,128)(2,1)}, bf16[192,1024]{1,0:T(8,128)(2,1)S(1)}, u32[]{:S(2)}, u32[]{:S(2)}) collective-permute-start(bf16[192,1024]{1,0:T(8,128)(2,1)} %refs_0_.3), channel_id=1, source_target_pairs={{0,6},{1,7},{2,0},{3,1},{4,2},{5,3},{6,4},{7,5},{8,14},{9,15},{10,... | collective-permute-start | bytes 1179656 | tf_op jit(solution)/shard_map/ppermute | solution.py:288
  5.3 11.2 %collective-permute-start = (bf16[192,1024]{1,0:T(8,128)(2,1)}, bf16[192,1024]{1,0:T(8,128)(2,1)}, u32[]{:S(2)}, u32[]{:S(2)}) collective-permute-start(bf16[192,1024]{1,0:T(8,128)(2,1)} %refs_0_.3), channel_id=1, source_target_pairs={{0,2},{1,3},{2,4},{3,5},{4,6},{5,7},{6,0},{7,1},{8,10},{9,11},{10,... | collective-permute-start | bytes 1179656 | tf_op jit(solution)/shard_map/ppermute | solution.py:288
  5.3 29.3 %collective-permute-start.5 = (bf16[64,1,2,64,128]{4,3,2,1,0:T(8,128)(2,1)}, bf16[64,1,2,64,128]{4,3,2,1,0:T(8,128)(2,1)S(1)}, u32[]{:S(2)}, u32[]{:S(2)}) collective-permute-start(bf16[64,1,2,64,128]{4,3,2,1,0:T(8,128)(2,1)} %refs_0_.5), channel_id=1, source_target_pairs={{0,8},{1,33},{2,10},{3,35},{4,12},{5,37},{6,14},{7,39},{8,16},{9,4... | collective-permute-start | bytes 6291464 | tf_op jit(solution)/shard_map/ppermute | solution.py:288
  6.5 28.1 %collective-permute-start.6 = (bf16[64,1,2,64,128]{4,3,2,1,0:T(8,128)(2,1)}, bf16[64,1,2,64,128]{4,3,2,1,0:T(8,128)(2,1)}, u32[]{:S(2)}, u32[]{:S(2)}) collective-permute-start(bf16[64,1,2,64,128]{4,3,2,1,0:T(8,128)(2,1)} %refs_0_.5), channel_id=1, source_target_pairs={{0,24},{1,97},{2,26},{3,99},{4,28},{5,101},{6,30},{7,103},{8,0},{9... | collective-permute-start | bytes 6291464 | tf_op jit(solution)/shard_map/ppermute | solution.py:288
  16.5 6.6 %collective-permute-start.4 = (s32[4,128]{1,0:T(4,128)S(1)}, s32[4,128]{1,0:T(4,128)S(1)}, u32[]{:S(2)}, u32[]{:S(2)}) collective-permute-start(s32[4,128]{1,0:T(4,128)S(1)} %pad_add_fusion.1), channel_id=1, source_target_pairs={{0,64},{1,17},{2,66},{3,19},{4,68},{5,21},{6,70},{7,23},{8,72},{9,... | collective-permute-start | bytes 6152 | tf_op jit(solution)/shard_map/ppermute | solution.py:288
  19.4 4.0 %collective-permute-start.3 = (s32[4,128]{1,0:T(4,128)S(1)}, s32[4,128]{1,0:T(4,128)S(1)}, u32[]{:S(2)}, u32[]{:S(2)}) collective-permute-start(s32[4,128]{1,0:T(4,128)S(1)} %pad_add_fusion.1), channel_id=1, source_target_pairs={{0,32},{1,9},{2,34},{3,11},{4,36},{5,13},{6,38},{7,15},{8,40},{9,1... | collective-permute-start | bytes 6152 | tf_op jit(solution)/shard_map/ppermute | solution.py:288
  19.8 4.8 %collective-permute-start.2 = (s32[4,128]{1,0:T(4,128)S(1)}, s32[4,128]{1,0:T(4,128)S(1)}, u32[]{:S(2)}, u32[]{:S(2)}) collective-permute-start(s32[4,128]{1,0:T(4,128)S(1)} %pad_add_fusion.1), channel_id=1, source_target_pairs={{0,96},{1,25},{2,98},{3,27},{4,100},{5,29},{6,102},{7,31},{8,104},... | collective-permute-start | bytes 6152 | tf_op jit(solution)/shard_map/ppermute | solution.py:288
  23.0 5.0 %collective-permute-start.9 = (bf16[96,1024]{1,0:T(8,128)(2,1)S(1)}, bf16[96,1024]{1,0:T(8,128)(2,1)S(1)}, u32[]{:S(2)}, u32[]{:S(2)}) collective-permute-start(bf16[96,1024]{1,0:T(8,128)(2,1)S(1)} %slice.49), channel_id=1, source_target_pairs={{0,6},{1,7},{2,0},{3,1},{4,2},{5,3},{6,4},{7,5},{8,14},{9,15},{10,... | collective-permute-start | bytes 589832 | tf_op jit(solution)/shard_map/ppermute | solution.py:288
  23.4 7.9 %collective-permute-start.7 = (bf16[96,1024]{1,0:T(8,128)(2,1)S(1)}, bf16[96,1024]{1,0:T(8,128)(2,1)S(1)}, u32[]{:S(2)}, u32[]{:S(2)}) collective-permute-start(bf16[96,1024]{1,0:T(8,128)(2,1)S(1)} %slice.48), channel_id=1, source_target_pairs={{0,2},{1,3},{2,4},{3,5},{4,6},{5,7},{6,0},{7,1},{8,10},{9,11},{10,... | collective-permute-start | bytes 589832 | tf_op jit(solution)/shard_map/ppermute | solution.py:288
  24.6 15.0 %collective-permute-start.13 = (bf16[192,1024]{1,0:T(8,128)(2,1)}, bf16[192,1024]{1,0:T(8,128)(2,1)S(1)}, u32[]{:S(2)}, u32[]{:S(2)}) collective-permute-start(bf16[192,1024]{1,0:T(8,128)(2,1)} %refs_0_.3), channel_id=1, source_target_pairs={{0,1},{1,0},{2,3},{3,2},{4,5},{5,4},{6,7},{7,6},{8,9},{9,8},{10,11... | collective-permute-start | bytes 1179656 | tf_op jit(solution)/shard_map/ppermute | solution.py:288
  28.0 5.1 %collective-permute-start.10 = (bf16[96,1024]{1,0:T(8,128)(2,1)S(1)}, bf16[96,1024]{1,0:T(8,128)(2,1)S(1)}, u32[]{:S(2)}, u32[]{:S(2)}) collective-permute-start(bf16[96,1024]{1,0:T(8,128)(2,1)S(1)} %collective-permute-done.9.refs_7_), channel_id=1, source_target_pairs={{0,1},{1,0},{2,3},{3,2},{4,5},{5,4},{6,7},{7,6},{8,9},{9,8},{10,11... | collective-permute-start | bytes 589832 | tf_op jit(solution)/shard_map/ppermute | solution.py:288
  31.3 2.9 %collective-permute-start.8 = (bf16[96,1024]{1,0:T(8,128)(2,1)S(1)}, bf16[96,1024]{1,0:T(8,128)(2,1)S(1)}, u32[]{:S(2)}, u32[]{:S(2)}) collective-permute-start(bf16[96,1024]{1,0:T(8,128)(2,1)S(1)} %collective-permute-done.7.refs_6_), channel_id=1, source_target_pairs={{0,1},{1,0},{2,3},{3,2},{4,5},{5,4},{6,7},{7,6},{8,9},{9,8},{10,11... | collective-permute-start | bytes 589832 | tf_op jit(solution)/shard_map/ppermute | solution.py:288
  33.1 6.1 %copy-start.10 = (pred[128,128]{1,0:T(8,128)(4,1)S(1)}, pred[128,128]{1,0:T(8,128)(4,1)}, u32[]{:S(2)}) copy-start(pred[128,128]{1,0:T(8,128)(4,1)} %iota_compare_fusion.1) | copy-start | bytes 49156
  33.1 6.4 %copy-start.4 = (bf16[8192,128]{1,0:T(8,128)(2,1)S(1)}, bf16[8192,128]{1,0:T(8,128)(2,1)}, u32[]{:S(2)}) copy-start(bf16[8192,128]{1,0:T(8,128)(2,1)} %refs_11_.1) | copy-start | bytes 6291460
  33.1 6.5 %copy-start.7 = (bf16[192,1024]{1,0:T(8,128)(2,1)S(1)}, bf16[192,1024]{1,0:T(8,128)(2,1)}, u32[]{:S(2)}) copy-start(bf16[192,1024]{1,0:T(8,128)(2,1)} %refs_0_.3) | copy-start | bytes 1179652
  33.2 6.4 %collective-permute-start.14 = (bf16[192,1024]{1,0:T(8,128)(2,1)}, bf16[192,1024]{1,0:T(8,128)(2,1)S(1)}, u32[]{:S(2)}, u32[]{:S(2)}) collective-permute-start(bf16[192,1024]{1,0:T(8,128)(2,1)} %collective-permute-done.refs_2_), channel_id=1, source_target_pairs={{0,1},{1,0},{2,3},{3,2},{4,5},{5,4},{6,7},{7,6},{8,9},{9,8},{10,11... | collective-permute-start | bytes 1179656 | tf_op jit(solution)/shard_map/ppermute | solution.py:288
  34.2 5.4 %collective-permute-start.15 = (bf16[192,1024]{1,0:T(8,128)(2,1)S(1)}, bf16[192,1024]{1,0:T(8,128)(2,1)S(1)}, u32[]{:S(2)}, u32[]{:S(2)}) collective-permute-start(bf16[192,1024]{1,0:T(8,128)(2,1)S(1)} %collective-permute-done.1.refs_3_), channel_id=1, source_target_pairs={{0,1},{1,0},{2,3},{3,2},{4,5},{5,4},{6,7},{7,6},{8,9},{9,8},{10,11... | collective-permute-start | bytes 1179656 | tf_op jit(solution)/shard_map/ppermute | solution.py:288
  34.7 32.2 %collective-permute-start.11 = (bf16[32,1,2,64,128]{4,3,2,1,0:T(8,128)(2,1)S(1)}, bf16[32,1,2,64,128]{4,3,2,1,0:T(8,128)(2,1)S(1)}, u32[]{:S(2)}, u32[]{:S(2)}) collective-permute-start(bf16[32,1,2,64,128]{4,3,2,1,0:T(8,128)(2,1)S(1)} %slice.46), channel_id=1, source_target_pairs={{0,8},{1,33},{2,10},{3,35},{4,12},{5,37},{6,14},{7,39},{8,16},{9,4... | collective-permute-start | bytes 3145736 | tf_op jit(solution)/shard_map/ppermute | solution.py:288
  36.1 30.8 %collective-permute-start.12 = (bf16[32,1,2,64,128]{4,3,2,1,0:T(8,128)(2,1)S(1)}, bf16[32,1,2,64,128]{4,3,2,1,0:T(8,128)(2,1)S(1)}, u32[]{:S(2)}, u32[]{:S(2)}) collective-permute-start(bf16[32,1,2,64,128]{4,3,2,1,0:T(8,128)(2,1)S(1)} %slice.47), channel_id=1, source_target_pairs={{0,24},{1,97},{2,26},{3,99},{4,28},{5,101},{6,30},{7,103},{8,0},{9... | collective-permute-start | bytes 3145736 | tf_op jit(solution)/shard_map/ppermute | solution.py:288
  39.6 27.3 %copy-start = (bf16[64,1,2,64,128]{4,3,2,1,0:T(8,128)(2,1)S(1)}, bf16[64,1,2,64,128]{4,3,2,1,0:T(8,128)(2,1)}, u32[]{:S(2)}) copy-start(bf16[64,1,2,64,128]{4,3,2,1,0:T(8,128)(2,1)} %refs_0_.5) | copy-start | bytes 6291460
  51.7 41.1 %copy-start.5 = (bf16[192,256]{1,0:T(8,128)(2,1)}, bf16[192,256]{1,0:T(8,128)(2,1)S(1)}, u32[]{:S(2)}) copy-start(bf16[192,256]{1,0:T(8,128)(2,1)S(1)} %get-tuple-element.20.refs_6_) | copy-start | bytes 294916
  51.7 41.1 %copy-start.8 = (bf16[192,1024]{1,0:T(8,128)(2,1)}, bf16[192,1024]{1,0:T(8,128)(2,1)S(1)}, u32[]{:S(2)}) copy-start(bf16[192,1024]{1,0:T(8,128)(2,1)S(1)} %get-tuple-element.19.refs_5_) | copy-start | bytes 1179652
  51.7 11.7 %collective-permute-start.16 = (bf16[192,1024]{1,0:T(8,128)(2,1)S(1)}, bf16[192,1024]{1,0:T(8,128)(2,1)S(1)}, u32[]{:S(2)}, u32[]{:S(2)}) collective-permute-start(bf16[192,1024]{1,0:T(8,128)(2,1)S(1)} %get-tuple-element.19.refs_5_), channel_id=1, source_target_pairs={{0,96},{1,25},{2,98},{3,27},{4,100},{5,29},{6,102},{7,31},{8,104},... | collective-permute-start | bytes 1179656 | tf_op jit(solution)/shard_map/ppermute | solution.py:288
  54.5 12.3 %collective-permute-start.17 = (bf16[192,1024]{1,0:T(8,128)(2,1)S(1)}, bf16[192,1024]{1,0:T(8,128)(2,1)S(1)}, u32[]{:S(2)}, u32[]{:S(2)}) collective-permute-start(bf16[192,1024]{1,0:T(8,128)(2,1)S(1)} %get-tuple-element.19.refs_5_), channel_id=1, source_target_pairs={{0,32},{1,9},{2,34},{3,11},{4,36},{5,13},{6,38},{7,15},{8,40},{9,1... | collective-permute-start | bytes 1179656 | tf_op jit(solution)/shard_map/ppermute | solution.py:288
  54.5 12.3 %collective-permute-start.18 = (bf16[192,1024]{1,0:T(8,128)(2,1)S(1)}, bf16[192,1024]{1,0:T(8,128)(2,1)S(1)}, u32[]{:S(2)}, u32[]{:S(2)}) collective-permute-start(bf16[192,1024]{1,0:T(8,128)(2,1)S(1)} %get-tuple-element.19.refs_5_), channel_id=1, source_target_pairs={{0,64},{1,17},{2,66},{3,19},{4,68},{5,21},{6,70},{7,23},{8,72},{9,... | collective-permute-start | bytes 1179656 | tf_op jit(solution)/shard_map/ppermute | solution.py:288
  66.9 25.9 %copy-start.2 = (bf16[32,1,2,64,128]{4,3,2,1,0:T(8,128)(2,1)}, bf16[32,1,2,64,128]{4,3,2,1,0:T(8,128)(2,1)S(1)}, u32[]{:S(2)}) copy-start(bf16[32,1,2,64,128]{4,3,2,1,0:T(8,128)(2,1)S(1)} %collective-permute-done.12.refs_4_) | copy-start | bytes 3145732
  92.8 21.2 %collective-permute-start.19 = (bf16[192,1152]{1,0:T(8,128)(2,1)}, bf16[192,1152]{1,0:T(8,128)(2,1)}, u32[]{:S(2)}, u32[]{:S(2)}) collective-permute-start(bf16[192,1152]{1,0:T(8,128)(2,1)} %get-tuple-element.23), channel_id=1, source_target_pairs={{0,32},{1,9},{2,34},{3,11},{4,36},{5,13},{6,38},{7,15},{8,40},{9,1... | collective-permute-start | bytes 1327112 | tf_op jit(solution)/shard_map/ppermute | solution.py:288
  92.9 21.1 %collective-permute-start.20 = (bf16[192,1152]{1,0:T(8,128)(2,1)}, bf16[192,1152]{1,0:T(8,128)(2,1)}, u32[]{:S(2)}, u32[]{:S(2)}) collective-permute-start(bf16[192,1152]{1,0:T(8,128)(2,1)} %get-tuple-element.24), channel_id=1, source_target_pairs={{0,96},{1,25},{2,98},{3,27},{4,100},{5,29},{6,102},{7,31},{8,104},... | collective-permute-start | bytes 1327112 | tf_op jit(solution)/shard_map/ppermute | solution.py:288
  95.5 18.4 %collective-permute-start.21 = (bf16[192,1152]{1,0:T(8,128)(2,1)}, bf16[192,1152]{1,0:T(8,128)(2,1)}, u32[]{:S(2)}, u32[]{:S(2)}) collective-permute-start(bf16[192,1152]{1,0:T(8,128)(2,1)} %get-tuple-element.25), channel_id=1, source_target_pairs={{0,64},{1,17},{2,66},{3,19},{4,68},{5,21},{6,70},{7,23},{8,72},{9,... | collective-permute-start | bytes 1327112 | tf_op jit(solution)/shard_map/ppermute | solution.py:288
  97.1 1.6 %copy-start.1 = (bf16[64,1,2,64,128]{4,3,2,1,0:T(8,128)(2,1)S(1)}, bf16[64,1,2,64,128]{4,3,2,1,0:T(8,128)(2,1)}, u32[]{:S(2)}) copy-start(bf16[64,1,2,64,128]{4,3,2,1,0:T(8,128)(2,1)} %refs_0_.5) | copy-start | bytes 6291460
  98.7 1.2 %copy-start.3 = (bf16[32,1,2,64,128]{4,3,2,1,0:T(8,128)(2,1)S(1)}, bf16[32,1,2,64,128]{4,3,2,1,0:T(8,128)(2,1)}, u32[]{:S(2)}) copy-start(bf16[32,1,2,64,128]{4,3,2,1,0:T(8,128)(2,1)} %copy-done.2) | copy-start | bytes 3145732
  99.9 0.9 copy-start.6
  100.8 1.0 copy-start.9

commit v2 on v1

v2 whole, which is shorter than its diff:
```python
import functools
import math

import jax
import jax.numpy as jnp
from jax import lax
from jax.experimental import pallas as pl
from jax.experimental.pallas import tpu as pltpu
from jax.sharding import PartitionSpec as P

HD = 128
SUF = 64
PAGE = 64
MAXP = 128
NODES = 3
GROUPS = 4
HEADS = 8
ROWS = HEADS * SUF
BLOCK = 8
KEYS = BLOCK * PAGE
FEATURES = 8192

rope_base = 500000.0
norm_eps = 1e-05
FACTOR = math.log2(math.e) / math.sqrt(HD)
LOW = -1e30

AX = ("pool", "tp")
EVERY = [(x, y, z, c) for x in range(4) for y in range(4) for z in range(4) for c in range(2)]


def flat(x, y, z, c):
    return ((x % 4) * 4 + y % 4) * 8 + (z % 4) * 2 + c


def page_shift(s):
    return [(flat(x, y, z, c), flat(x + s * c, y + s * (1 - c), z, c)) for x, y, z, c in EVERY]


def query_shift(s):
    return [(flat(x, y, z, c), flat(x + s * (1 - c), y + s * c, z, c)) for x, y, z, c in EVERY]


def z_shift(s):
    return [(flat(x, y, z, c), flat(x, y, z + s, c)) for x, y, z, c in EVERY]


def core_swap():
    return [(flat(x, y, z, c), flat(x, y, z, 1 - c)) for x, y, z, c in EVERY]


def project_kernel(shape, ranks, *refs):
    refs = list(refs)
    xs = [[refs.pop(0) for _ in range(n)] for n in shape]
    load = lambda group: jnp.concatenate([r[...] for r in group], axis=0).astype(jnp.float32)
    (wq, wk, wv, cos, sin, tails), refs = refs[:6], refs[6:]
    sends, (q_out, kv_out, w_s, x_s, sems) = refs[:3], refs[3:]

    copies = []
    for t in range(4):
        copies.append([pltpu.make_async_copy(wq.at[:, pl.ds(t * 256, 256)], w_s.at[t], sems.at[t])])
    copies.append(
        [
            pltpu.make_async_copy(wk, w_s.at[4, :, pl.ds(0, 128)], sems.at[4]),
            pltpu.make_async_copy(wv, w_s.at[4, :, pl.ds(128, 128)], sems.at[5]),
        ]
    )
    for some in copies:
        for copy in some:
            copy.start()
    for k, send in enumerate(sends):
        send[:, HD:] = tails[k]
    total = jnp.zeros((192, 128), jnp.float32)
    for x in xs:
        wide = load(x)
        for k in range(8):
            part = wide[:, k * 128 : (k + 1) * 128]
            total = total + part * part
    scale = lax.rsqrt(jnp.sum(total, axis=-1, keepdims=True) * (1.0 / FEATURES) + norm_eps)
    for i, x in enumerate(xs):
        x_s[ranks[i]] = (load(x) * scale).astype(jnp.bfloat16)
    for t, some in enumerate(copies):
        for copy in some:
            copy.wait()
        total = None
        for r in range(8):
            part = jnp.dot(x_s[r], w_s[t, r * 1024 : (r + 1) * 1024, :], preferred_element_type=jnp.float32)
            total = part if total is None else total + part
        turned = []
        for h in range(2):
            u = total[:, h * HD : (h + 1) * HD]
            g = t * 2 + h
            if g <= HEADS:
                u = u * cos[...] + pltpu.roll(u, 64, 1) * sin[...]
            if g < HEADS:
                turned.append(u)
            else:
                kv_out[:, (g - HEADS) * HD : (g - HEADS + 1) * HD] = u.astype(jnp.bfloat16)
        if turned:
            for n in range(NODES):
                both = jnp.concatenate([u[n * SUF : (n + 1) * SUF] for u in turned], axis=0).T.astype(jnp.bfloat16)
                q_out[n, :, t * 128 : (t + 1) * 128] = both
                for send in sends:
                    send[n, :HD, t * 128 : (t + 1) * 128] = both


def project(xs, ranks, wq, wk, wv, rope, tails):
    vmem = pl.BlockSpec(memory_space=pltpu.VMEM)
    hbm = pl.BlockSpec(memory_space=pltpu.HBM)
    bf16 = jnp.bfloat16
    outs = [jax.ShapeDtypeStruct((NODES, HD + 16, ROWS), bf16)] * 3
    outs += [jax.ShapeDtypeStruct((NODES, HD, ROWS), bf16), jax.ShapeDtypeStruct((192, 256), bf16)]
    shape = tuple(len(g) for g in xs)
    xs = [a for g in xs for a in g]
    return pl.pallas_call(
        functools.partial(project_kernel, shape),
        out_shape=outs,
        in_specs=[pl.BlockSpec(memory_space=pltpu.SMEM)] + [vmem] * len(xs) + [hbm] * 3 + [vmem] * 3,
        out_specs=[vmem] * 5,
        scratch_shapes=[
            pltpu.VMEM((5, FEATURES, 256), bf16),
            pltpu.VMEM((8, 192, 1024), bf16),
            pltpu.SemaphoreType.DMA((6,)),
        ],
        compiler_params=pltpu.CompilerParams(vmem_limit_bytes=48 * 2**20),
        cost_estimate=pl.CostEstimate(flops=10**6, bytes_accessed=10**6, transcendentals=0),
    )(jnp.stack(ranks).astype(jnp.int32), *xs, wq, wk, wv, *rope, tails)


def attend_kernel(groups, plan, idx, steps, keys, *refs):
    refs = list(refs)
    take = lambda n: [refs.pop(0) for _ in range(n)]
    pages = take(len(plan))
    qs = take(len(groups))
    own = groups == (3,)
    suffix = take(1)[0] if own else None
    outs = [take(2 if own else 1) for _ in groups]
    pool, q_s, s_a, s_b, acc_s, sems = refs

    copies = []
    for i, (at, ref) in enumerate(zip(plan, pages)):
        copies.append(pltpu.make_async_copy(ref.at[:, 0], pool.at[pl.ds(at, ref.shape[0])], sems.at[i]))
    for copy in copies:
        copy.start()
    for k, q in enumerate(qs):
        q_s[k * NODES : (k + 1) * NODES] = q[:, :HD]
    for copy in copies:
        copy.wait()

    place = lax.broadcasted_iota(jnp.int32, (PAGE, 1), 0)
    over_keys = (((0,), (0,)), ((), ()))
    nodes = len(groups) * NODES

    def scores(n, i, s_ref):
        k = jnp.concatenate([pool[idx[n, i * BLOCK + u], 0] for u in range(BLOCK)], axis=0)
        s_ref[...] = jnp.dot(k, q_s[n], preferred_element_type=jnp.float32)

    def mask(n, i, s_ref):
        left = keys[n] - i * KEYS
        for u in range(BLOCK):

            @pl.when(left < (u + 1) * PAGE)
            def _():
                rows = slice(u * PAGE, (u + 1) * PAGE)
                s_ref[rows] = jnp.where(place < left - u * PAGE, s_ref[rows], LOW)

    def values(n, i, s_ref, peak, total):
        v = jnp.concatenate([pool[idx[n, i * BLOCK + u], 1] for u in range(BLOCK)], axis=0)
        s = s_ref[...]
        old = jnp.where(i == 0, LOW, peak)
        peak = jnp.maximum(old, jnp.max(jnp.max(s.reshape(-1, 8, ROWS), axis=0), axis=0, keepdims=True))
        keep = jnp.exp2((old - peak) * FACTOR)
        w = jnp.exp2(s * FACTOR - peak * FACTOR)
        total = total * keep + jnp.sum(w.reshape(-1, 8, ROWS), axis=0)
        acc_s[...] = acc_s[...] * keep + lax.dot_general(
            v, w.astype(jnp.bfloat16), over_keys, preferred_element_type=jnp.float32
        )
        return peak, total

    def finish(n, peak, total):
        total = jnp.sum(total, axis=0, keepdims=True)
        out = acc_s[...]
        if own:
            r = pl.ds(pl.multiple_of(n * SUF, SUF), SUF)
            s = jnp.dot(suffix[r, :HD], q_s[n], preferred_element_type=jnp.float32)
            key = lax.broadcasted_iota(jnp.int32, (SUF, ROWS), 0)
            query = lax.broadcasted_iota(jnp.int32, (SUF, ROWS), 1) % SUF
            s = jnp.where(key <= query, s, LOW)
            old = peak
            peak = jnp.maximum(jnp.max(s, axis=0, keepdims=True), old)
            keep = jnp.exp2((old - peak) * FACTOR)
            w = jnp.exp2((s - peak) * FACTOR)
            new = lax.dot_general(suffix[r, HD:], w.astype(jnp.bfloat16), over_keys, preferred_element_type=jnp.float32)
            out = out * keep + new
            total = total * keep + jnp.sum(w, axis=0, keepdims=True)
        level = peak * FACTOR + jnp.log2(total)
        out = out * (1.0 / total)
        if own:
            outs[0][0][n] = out
            outs[0][1][n] = jnp.broadcast_to(level, (8, ROWS))
        else:
            high = level.astype(jnp.bfloat16).astype(jnp.float32)
            rest = level - high
            mid = rest.astype(jnp.bfloat16).astype(jnp.float32)
            at = lax.broadcasted_iota(jnp.int32, (16, ROWS), 0)
            tile = jnp.where(at == 0, high, jnp.where(at == 1, mid, jnp.where(at == 2, rest - mid, 0.0)))
            for k in range(len(groups)):

                @pl.when((n >= k * NODES) & (n < (k + 1) * NODES))
                def _():
                    outs[k][0][n - k * NODES, :HD] = out.astype(jnp.bfloat16)
                    outs[k][0][n - k * NODES, HD:] = tile.astype(jnp.bfloat16)

    def after(n, i):
        more = (i + 1 < steps[n]) | (n == nodes - 1)
        return jnp.where(more, n, n + 1), jnp.where(more, i + 1, 0)

    def one(n, i, now, later, peak, total):
        n_next, i_next = after(n, i)
        scores(n_next, jnp.minimum(i_next, MAXP // BLOCK - 1), later)
        peak, total = values(n, jnp.minimum(i, MAXP // BLOCK - 1), now, peak, total)

        @pl.when(i == steps[n] - 1)
        def _():
            finish(n, peak, total)

        @pl.when(i_next >= steps[n_next] - 1)
        def _():
            mask(n_next, i_next, later)

        return n_next, i_next, peak, total

    def two(_, state):
        n, i, peak, total = state
        n, i, peak, total = one(n, i, s_a, s_b, peak, total)
        return one(n, i, s_b, s_a, peak, total)

    acc_s[...] = jnp.zeros_like(acc_s)
    scores(0, 0, s_a)
    mask(0, 0, s_a)
    count = lax.fori_loop(0, nodes, lambda n, c: c + steps[n], 0)
    zero = jnp.int32(0)
    lax.fori_loop(
        0, (count + 1) // 2, two, (zero, zero, jnp.full((1, ROWS), LOW, jnp.float32), jnp.zeros((8, ROWS), jnp.float32))
    )


def attend(groups, lists, pages, qs, suffix):
    own = groups == (3,)
    f32 = jnp.float32
    if own:
        outs = [jax.ShapeDtypeStruct((NODES, HD, ROWS), f32), jax.ShapeDtypeStruct((NODES, 8, ROWS), f32)]
    else:
        outs = [jax.ShapeDtypeStruct((NODES, HD + 16, ROWS), jnp.bfloat16) for _ in groups]
    n = len(groups) * NODES
    extra = [suffix] if own else []
    vmem = pl.BlockSpec(memory_space=pltpu.VMEM)
    smem = pl.BlockSpec(memory_space=pltpu.SMEM)
    hbm = pl.BlockSpec(memory_space=pl.ANY)
    return pl.pallas_call(
        functools.partial(attend_kernel, groups, tuple(at for at, _ in pages)),
        out_shape=outs,
        in_specs=[smem] * 3 + [hbm] * len(pages) + [vmem] * (len(qs) + len(extra)),
        out_specs=[vmem] * len(outs),
        scratch_shapes=[
            pltpu.VMEM((sum(a.shape[0] for _, a in pages), 2, PAGE, HD), jnp.bfloat16),
            pltpu.VMEM((n, HD, ROWS), jnp.bfloat16),
            pltpu.VMEM((KEYS, ROWS), f32),
            pltpu.VMEM((KEYS, ROWS), f32),
            pltpu.VMEM((HD, ROWS), f32),
            pltpu.SemaphoreType.DMA((len(pages),)),
        ],
        compiler_params=pltpu.CompilerParams(vmem_limit_bytes=(52 if own else 36) * 2**20),
        cost_estimate=pl.CostEstimate(flops=10**9, bytes_accessed=10**6, transcendentals=0),
    )(*lists, *[a for _, a in pages], *qs, *extra)


def merge_kernel(o_ref, l_ref, a_ref, b_ref, c_ref, out_ref):
    others = [a_ref, b_ref, c_ref]
    for n in range(NODES):
        levels = [l_ref[n, :1]]
        for r in others:
            t = r[n, HD:].astype(jnp.float32)
            levels.append(t[0:1] + t[1:2] + t[2:3])
        top = functools.reduce(jnp.maximum, levels)
        weights = [jnp.exp2(v - top) for v in levels]
        share = 1.0 / functools.reduce(jnp.add, weights)
        out = o_ref[n] * (weights[0] * share)
        for w, r in zip(weights[1:], others):
            out = out + r[n, :HD].astype(jnp.float32) * (w * share)
        rows = slice(n * SUF, (n + 1) * SUF)
        for t in range(HEADS // 2):
            both = out[:, t * 128 : (t + 1) * 128].T.astype(jnp.bfloat16)
            out_ref[rows, 2 * t * HD : (2 * t + 1) * HD] = both[:SUF]
            out_ref[rows, (2 * t + 1) * HD : (2 * t + 2) * HD] = both[SUF:]


def make_lists(mask, where, lens):
    place = jnp.arange(MAXP, dtype=jnp.int32)
    upto = jnp.sum(jnp.where(place[None, None, :] <= place[None, :, None], mask[:, None, :], False).astype(jnp.int32), axis=-1)
    hit = mask[:, None, :] & (upto[:, None, :] - 1 == place[None, :, None])
    idx = jnp.sum(jnp.where(hit, where[:, None, :], 0), axis=-1)
    count = jnp.sum(mask.astype(jnp.int32), axis=-1)
    keys = jnp.sum(jnp.where(mask, jnp.minimum(PAGE, lens[:, None] - place[None, :] * PAGE), 0), axis=-1)
    return idx, jnp.maximum((count + BLOCK - 1) // BLOCK, 1), keys


def body(tokens, w_query, w_key, w_value, kv_pool, page_owner, page_slot, prefix_len):
    pool_at, tp_at = lax.axis_index("pool"), lax.axis_index("tp")
    x, y, core = pool_at // 4, pool_at % 4, tp_at % 2
    along_page = jnp.where(core == 0, y, x)
    along_query = jnp.where(core == 0, x, y)
    move = lambda a, perm: lax.ppermute(a, AX, perm)

    tok_a, tok_b = move(tokens, z_shift(1)), move(tokens, z_shift(-1))
    tok_o = move(tokens, core_swap())
    page_a, page_b = move(kv_pool, page_shift(1)), move(kv_pool, page_shift(-1))

    positions = (prefix_len[:, None] + jnp.arange(SUF, dtype=jnp.int32)[None, :]).astype(jnp.float32).reshape(192, 1)
    inverse = rope_base ** (-(jnp.arange(HD // 2, dtype=jnp.float32) * 2.0 / HD))
    angles = positions * inverse
    cosine, sine = jnp.cos(angles), jnp.sin(angles)
    rope = (jnp.concatenate([cosine, cosine], axis=1), jnp.concatenate([-sine, sine], axis=1))

    owner = page_owner[..., 0]
    owner_page = jnp.where(core == 0, owner % 4, owner // 4)
    owner_query = jnp.where(core == 0, owner // 4, owner % 4)
    apart = (owner_page - along_page) % 4
    start = jnp.where(apart == 0, 0, jnp.where(apart == 3, 64, jnp.where(apart == 1, 128, 192)))
    valid = jnp.arange(MAXP, dtype=jnp.int32)[None, :] * PAGE < prefix_len[:, None]
    masks = jnp.concatenate([valid & (owner_query == (along_query + d) % 4) for d in (1, -1, 2, 0)], axis=0)
    idx, steps, keys = make_lists(masks, jnp.tile(start + page_slot, (4, 1)), jnp.tile(prefix_len, 4))
    numbers = jnp.stack([steps, keys // 64, keys % 64], axis=-1)
    tails = jnp.zeros((9, 16, ROWS), jnp.bfloat16)
    tails = tails.at[:, 0, :MAXP].set(idx[:9].astype(jnp.bfloat16)).at[:, 1, :3].set(numbers[:9].astype(jnp.bfloat16))
    tails = tails.reshape(3, NODES, 16, ROWS)

    tok_a, tok_b, tails, rope = lax.optimization_barrier((tok_a, tok_b, tails, rope))
    tok_ao, tok_bo = move(tok_a, core_swap()), move(tok_b, core_swap())
    tok_c, tok_d = move(tok_a[:96], z_shift(1)), move(tok_b[96:], z_shift(-1))
    tok_co, tok_do = move(tok_c, core_swap()), move(tok_d, core_swap())
    z = tp_at // 2
    rank = lambda dz, same: ((z + dz) % 4) * 2 + (core if same else 1 - core)
    blocks = [[tokens], [tok_o], [tok_a], [tok_b], [tok_ao], [tok_bo], [tok_c, tok_d], [tok_co, tok_do]]
    ranks = [rank(dz, same) for dz, same in ((0, 1), (0, 0), (-1, 1), (1, 1), (-1, 0), (1, 0), (2, 1), (2, 0))]
    *sends, queries, suffix = project(blocks, ranks, w_query, w_key, w_value, rope, tails)
    suffix_kv = suffix.reshape(192, 2, 1, HD)

    page_a, page_b, suffix = lax.optimization_barrier((page_a, page_b, suffix))
    page_c, page_d = move(page_a[:32], page_shift(1)), move(page_b[32:], page_shift(-1))
    qs = [move(sends[1], query_shift(-1)), move(sends[0], query_shift(1)), move(sends[2], query_shift(2))]
    got = jnp.concatenate([q[:, HD : HD + 2, :MAXP] for q in qs], axis=0).astype(jnp.int32)
    theirs = (got[:, 0], got[:, 1, 0], got[:, 1, 1] * 64 + got[:, 1, 2])
    pages = ((0, kv_pool), (64, page_a), (128, page_b), (192, page_c), (224, page_d))
    sent = attend((0, 1, 2), theirs, pages, qs, None)
    back = [move(r, query_shift(s)) for r, s in zip(sent, (1, -1, 2))]
    mine = attend((3,), (idx[9:], steps[9:], keys[9:]), pages, [queries], suffix)
    attended = pl.pallas_call(
        merge_kernel,
        out_shape=jax.ShapeDtypeStruct((192, 1024), jnp.bfloat16),
        compiler_params=pltpu.CompilerParams(vmem_limit_bytes=16 * 2**20),
    )(*mine, *back)
    return attended, suffix_kv


def solution(mesh):
    in_specs = (
        P("pool", "tp"),
        P(None, "tp"),
        P(None, "tp"),
        P(None, "tp"),
        P("pool", "tp", None, None, None),
        P("pool", None, None),
        P("pool", None),
        P("pool"),
    )
    out_specs = (P("pool", "tp"), P("pool", None, "tp", None))
    return jax.shard_map(body, mesh=mesh, in_specs=in_specs, out_specs=out_specs, check_vma=False)
```

time: 118 us -> 109 us (0.924)
  Pallas kernels: 53.2 us -> 41.4 us
  waiting for transfers between devices: 16.8 us -> 24.8 us
  starting transfers between devices: 33.2 us -> 25.7 us
  other arithmetic: 3.47 us -> 6.44 us
  local copies, waits for them, and re-layouts: 9.5 us -> 8.15 us
    pallas_call x2, Pallas kernels: 38 us -> 27.4 us  [attend(): pl.pallas_call(functools.partial(attend_kernel, groups, tuple((at for at,...]
    ppermute x22 -> x19, waiting for transfers between devices: 16.8 us -> 24.8 us  [body(): move = lambda a, perm: lax.ppermute(a, AX, perm)]
    ppermute x22 -> x19, starting transfers between devices: 33.2 us -> 25.7 us  [body(): move = lambda a, perm: lax.ppermute(a, AX, perm)]
    pallas_call x1, Pallas kernels: 3.13 us -> 1.24 us  [body(): pl.pallas_call(merge_kernel, out_shape=jax.ShapeDtypeStruct((192, 1024),...]
    and x0 -> x2, other arithmetic: none -> 1.5 us  [body(): valid & (owner_query == (along_query + d) % 4)]
    unnamed x22 -> x19, local copies, waits for them, and re-layouts: 4.73 us -> 3.62 us
  transfers between devices with their start and end apart: 22 -> 19, of which waited for: 7 -> 6; matrix products, arithmetic and copies ran while one was open for 7% -> 10% of each run, Pallas kernels for 21% -> 22%
where the time goes in v2:
time: 109 us; the launch traced here: 108 us
  Pallas kernels  41.4 us (38%)
  starting transfers between devices  25.7 us (24%)
  waiting for transfers between devices  24.8 us (23%)
  local copies, waits for them, and re-layouts  8.15 us (7%)
  other arithmetic  6.44 us (6%)
    pallas_call x2, Pallas kernels, attend(): pl.pallas_call(functools.partial(attend_kernel, groups, tuple((at for at,...  27.4 us
    ppermute x19, starting transfers between devices, body(): move = lambda a, perm: lax.ppermute(a, AX, perm)  25.7 us
    ppermute x19, waiting for transfers between devices, body(): move = lambda a, perm: lax.ppermute(a, AX, perm)  24.8 us
    pallas_call x1, Pallas kernels, project(): pl.pallas_call(functools.partial(project_kernel, shape), out_shape=outs,...  12.8 us
    unnamed x19, local copies, waits for them, and re-layouts  3.62 us
    slice x1, local copies, waits for them, and re-layouts, body(): page_b[32:]  2.26 us
  transfers between devices with their start and end apart: 19, of which 6 were waited for; matrix products, arithmetic and copies ran while one was open for 10% of the time, Pallas kernels for 22%

profile of v2, /device:TPU:1, one launch (start us, length us, event | category | flops | bytes accessed | tf_op | source)
XLA Modules:
  0.0 107.6 jit_solution(8556435276738829483)
XLA Ops:
  0.6 2.5 %collective-permute-start.3 = (bf16[192,1024]{1,0:T(8,128)(2,1)}, bf16[192,1024]{1,0:T(8,128)(2,1)S(1)}, u32[]{:S(2)}, u32[]{:S(2)}) collective-permute-start(bf16[192,1024]{1,0:T(8,128)(2,1)} %refs_0_.3), channel_id=1, source_target_pairs={{0,2},{1,3},{2,4},{3,5},{4,6},{5,7},{6,0},{7,1},{8,10},{9,11},{10,... | collective-permute-start | bytes 1179656 | tf_op jit(solution)/shard_map/ppermute | solution.py:313
  3.2 2.2 %collective-permute-start.4 = (bf16[192,1024]{1,0:T(8,128)(2,1)}, bf16[192,1024]{1,0:T(8,128)(2,1)S(1)}, u32[]{:S(2)}, u32[]{:S(2)}) collective-permute-start(bf16[192,1024]{1,0:T(8,128)(2,1)} %refs_0_.3), channel_id=1, source_target_pairs={{0,6},{1,7},{2,0},{3,1},{4,2},{5,3},{6,4},{7,5},{8,14},{9,15},{10,... | collective-permute-start | bytes 1179656 | tf_op jit(solution)/shard_map/ppermute | solution.py:313
  5.4 1.0 collective-permute-start.2
  6.3 1.2 %collective-permute-start = (bf16[64,1,2,64,128]{4,3,2,1,0:T(8,128)(2,1)}, bf16[64,1,2,64,128]{4,3,2,1,0:T(8,128)(2,1)S(1)}, u32[]{:S(2)}, u32[]{:S(2)}) collective-permute-start(bf16[64,1,2,64,128]{4,3,2,1,0:T(8,128)(2,1)} %refs_0_.5), channel_id=1, source_target_pairs={{0,8},{1,33},{2,10},{3,35},{4,12},{5,37},{6,14},{7,39},{8,16},{9,4... | collective-permute-start | bytes 6291464 | tf_op jit(solution)/shard_map/ppermute | solution.py:313
  7.5 1.5 %collective-permute-start.1 = (bf16[64,1,2,64,128]{4,3,2,1,0:T(8,128)(2,1)}, bf16[64,1,2,64,128]{4,3,2,1,0:T(8,128)(2,1)}, u32[]{:S(2)}, u32[]{:S(2)}) collective-permute-start(bf16[64,1,2,64,128]{4,3,2,1,0:T(8,128)(2,1)} %refs_0_.5), channel_id=1, source_target_pairs={{0,24},{1,97},{2,26},{3,99},{4,28},{5,101},{6,30},{7,103},{8,0},{9... | collective-permute-start | bytes 6291464 | tf_op jit(solution)/shard_map/ppermute | solution.py:313
  9.0 0.7 add_convert_fusion
  9.8 0.7 tile.16
  10.4 0.1 sub.72
  10.5 0.8 compare_and_fusion.3
  11.3 0.7 compare_and_fusion.2
  12.0 0.2 select_reduce_fusion.1
  12.2 0.3 convert_reduce_fusion
  12.5 0.7 select_add_fusion
  13.2 0.1 convert_element_type.24
  13.3 0.3 select_reduce_fusion
  13.7 1.1 fusion.1
  14.8 0.1 copy.16
  14.9 0.2 scatter.9
  15.1 0.1 copy.17
  15.2 1.1 %pad_maximum_fusion = (f32[192,128]{1,0:T(8,128)S(1)}, f32[192,128]{1,0:T(8,128)S(1)}) fusion(f32[192,64]{1,0:T(8,128)} %get-tuple-element.80, f32[192,64]{1,0:T(8,128)S(1)} %get-tuple-element.79, f32[192,64]{1,0:T(8,128)S(1)} %get-tuple-element.78), kind=kLoop, calls=%fused_computation.6 | loop fusion | flops 49152 | bytes 344064 | tf_op jit(solution)/shard_map/concatenate | solution.py:323
  16.3 0.0 collective-permute-done.3.refs_2_
  16.3 0.0 collective-permute-done.4.refs_3_
  16.3 1.7 %collective-permute-start.8 = (bf16[96,1024]{1,0:T(8,128)(2,1)S(1)}, bf16[96,1024]{1,0:T(8,128)(2,1)S(1)}, u32[]{:S(2)}, u32[]{:S(2)}) collective-permute-start(bf16[96,1024]{1,0:T(8,128)(2,1)S(1)} %slice.105), channel_id=1, source_target_pairs={{0,6},{1,7},{2,0},{3,1},{4,2},{5,3},{6,4},{7,5},{8,14},{9,15},{10,... | collective-permute-start | bytes 589832 | tf_op jit(solution)/shard_map/ppermute | solution.py:313
  18.1 0.1 collective-permute-start.7
  18.1 4.2 %collective-permute-done.8.refs_7_ = bf16[96,1024]{1,0:T(8,128)(2,1)S(1)} collective-permute-done((bf16[96,1024]{1,0:T(8,128)(2,1)S(1)}, bf16[96,1024]{1,0:T(8,128)(2,1)S(1)}, u32[]{:S(2)}, u32[]{:S(2)}) %collective-permute-start.8) | collective-permute-done | bytes 196640 | tf_op jit(solution)/shard_map/ppermute | solution.py:313
  22.4 1.3 %collective-permute-start.10 = (bf16[96,1024]{1,0:T(8,128)(2,1)S(1)}, bf16[96,1024]{1,0:T(8,128)(2,1)S(1)}, u32[]{:S(2)}, u32[]{:S(2)}) collective-permute-start(bf16[96,1024]{1,0:T(8,128)(2,1)S(1)} %collective-permute-done.8.refs_7_), channel_id=1, source_target_pairs={{0,1},{1,0},{2,3},{3,2},{4,5},{5,4},{6,7},{7,6},{8,9},{9,8},{10,11... | collective-permute-start | bytes 589832 | tf_op jit(solution)/shard_map/ppermute | solution.py:313
  23.7 0.0 collective-permute-done.2.refs_1_
  23.7 0.0 collective-permute-start.5
  23.7 1.3 %collective-permute-done.7.refs_6_ = bf16[96,1024]{1,0:T(8,128)(2,1)} collective-permute-done((bf16[96,1024]{1,0:T(8,128)(2,1)S(1)}, bf16[96,1024]{1,0:T(8,128)(2,1)}, u32[]{:S(2)}, u32[]{:S(2)}) %collective-permute-start.7) | collective-permute-done | bytes 196640 | tf_op jit(solution)/shard_map/ppermute | solution.py:313
  25.0 1.7 %collective-permute-start.6 = (bf16[192,1024]{1,0:T(8,128)(2,1)S(1)}, bf16[192,1024]{1,0:T(8,128)(2,1)}, u32[]{:S(2)}, u32[]{:S(2)}) collective-permute-start(bf16[192,1024]{1,0:T(8,128)(2,1)S(1)} %collective-permute-done.4.refs_3_), channel_id=1, source_target_pairs={{0,1},{1,0},{2,3},{3,2},{4,5},{5,4},{6,7},{7,6},{8,9},{9,8},{10,11... | collective-permute-start | bytes 1179656 | tf_op jit(solution)/shard_map/ppermute | solution.py:313
  26.8 0.7 copy-done.7
  27.4 0.0 collective-permute-start.9
  27.4 0.1 stack.42.ranks
  27.5 1.7 %collective-permute-done.9.refs_8_ = bf16[96,1024]{1,0:T(8,128)(2,1)} collective-permute-done((bf16[96,1024]{1,0:T(8,128)(2,1)}, bf16[96,1024]{1,0:T(8,128)(2,1)}, u32[]{:S(2)}, u32[]{:S(2)}) %collective-permute-start.9) | collective-permute-done | bytes 196640 | tf_op jit(solution)/shard_map/ppermute | solution.py:313
  29.2 0.0 collective-permute-done.5.refs_4_
  29.2 0.0 collective-permute-done.6.refs_5_
  29.2 1.0 copy-done.6
  30.2 0.9 copy-done.8
  31.2 12.8 %shard_map.95 = (bf16[3,144,512]{2,1,0:T(8,128)(2,1)S(1)}, bf16[3,144,512]{2,1,0:T(8,128)(2,1)S(1)}, bf16[3,144,512]{2,1,0:T(8,128)(2,1)S(1)}, bf16[3,128,512]{2,1,0:T(8,128)(2,1)S(1)}, bf16[192,256]{1,0:T(8,128)(2,1)S(1)}) custom-call(s32[8]{0:T(128)S(1)} %stack.42.ranks, bf16[192,1024]{1,0:T(8,128)(2,1)S(1)} %copy-done.6, ...), custom_call_target="tpu_custom_call" | custom-call | flops 1000000 | bytes 1000000 | tf_op jit(solution)/shard_map/pallas_call | solution.py:115
  43.9 0.0 copy-start.4
  44.0 0.0 copy-start.1
  44.0 0.1 slice.106
  44.1 0.5 collective-permute-start.11
  44.5 2.3 %slice.107 = bf16[32,1,2,64,128]{4,3,2,1,0:T(8,128)(2,1)S(1)} slice(bf16[64,1,2,64,128]{4,3,2,1,0:T(8,128)(2,1)} %collective-permute-done.1.refs_2_), slice={[32:64], [0:1], [0:2], [0:64], [0:128]} | slice | bytes 2097152 | tf_op jit(solution)/shard_map/slice | solution.py:350
  46.8 1.7 %collective-permute-start.12 = (bf16[32,1,2,64,128]{4,3,2,1,0:T(8,128)(2,1)S(1)}, bf16[32,1,2,64,128]{4,3,2,1,0:T(8,128)(2,1)S(1)}, u32[]{:S(2)}, u32[]{:S(2)}) collective-permute-start(bf16[32,1,2,64,128]{4,3,2,1,0:T(8,128)(2,1)S(1)} %slice.107), channel_id=1, source_target_pairs={{0,24},{1,97},{2,26},{3,99},{4,28},{5,101},{6,30},{7,103},{8,0},{9... | collective-permute-start | bytes 3145736 | tf_op jit(solution)/shard_map/ppermute | solution.py:313
  48.6 2.5 %collective-permute-start.13 = (bf16[3,144,512]{2,1,0:T(8,128)(2,1)S(1)}, bf16[3,144,512]{2,1,0:T(8,128)(2,1)S(1)}, u32[]{:S(2)}, u32[]{:S(2)}) collective-permute-start(bf16[3,144,512]{2,1,0:T(8,128)(2,1)S(1)} %get-tuple-element.56), channel_id=1, source_target_pairs={{0,96},{1,25},{2,98},{3,27},{4,100},{5,29},{6,102},{7,31},{8,104},... | collective-permute-start | bytes 1327112 | tf_op jit(solution)/shard_map/ppermute | solution.py:313
  51.1 0.0 collective-permute-start.14
  51.1 1.6 %collective-permute-start.15 = (bf16[3,144,512]{2,1,0:T(8,128)(2,1)S(1)}, bf16[3,144,512]{2,1,0:T(8,128)(2,1)S(1)}, u32[]{:S(2)}, u32[]{:S(2)}) collective-permute-start(bf16[3,144,512]{2,1,0:T(8,128)(2,1)S(1)} %get-tuple-element.58), channel_id=1, source_target_pairs={{0,64},{1,17},{2,66},{3,19},{4,68},{5,21},{6,70},{7,23},{8,72},{9,... | collective-permute-start | bytes 1327112 | tf_op jit(solution)/shard_map/ppermute | solution.py:313
  52.7 9.2 %collective-permute-done.13.refs_5_ = bf16[3,144,512]{2,1,0:T(8,128)(2,1)S(1)} collective-permute-done((bf16[3,144,512]{2,1,0:T(8,128)(2,1)S(1)}, bf16[3,144,512]{2,1,0:T(8,128)(2,1)S(1)}, u32[]{:S(2)}, u32[]{:S(2)}) %collective-permute-start.13) | collective-permute-done | bytes 442400 | tf_op jit(solution)/shard_map/ppermute | solution.py:313
  61.9 3.6 %collective-permute-done.14.refs_6_ = bf16[3,144,512]{2,1,0:T(8,128)(2,1)S(1)} collective-permute-done((bf16[3,144,512]{2,1,0:T(8,128)(2,1)S(1)}, bf16[3,144,512]{2,1,0:T(8,128)(2,1)S(1)}, u32[]{:S(2)}, u32[]{:S(2)}) %collective-permute-start.14) | collective-permute-done | bytes 442400 | tf_op jit(solution)/shard_map/ppermute | solution.py:313
  65.6 4.7 %collective-permute-done.15.refs_7_ = bf16[3,144,512]{2,1,0:T(8,128)(2,1)S(1)} collective-permute-done((bf16[3,144,512]{2,1,0:T(8,128)(2,1)S(1)}, bf16[3,144,512]{2,1,0:T(8,128)(2,1)S(1)}, u32[]{:S(2)}, u32[]{:S(2)}) %collective-permute-start.15) | collective-permute-done | bytes 442400 | tf_op jit(solution)/shard_map/ppermute | solution.py:313
  70.4 0.5 fusion.2
  70.9 0.0 collective-permute-done.12.refs_4_
  70.9 16.9 %shard_map.97 = (bf16[3,144,512]{2,1,0:T(8,128)(2,1)}, bf16[3,144,512]{2,1,0:T(8,128)(2,1)}, bf16[3,144,512]{2,1,0:T(8,128)(2,1)}) custom-call(s32[9,128]{1,0:T(8,128)S(1)} %bitcast.72, s32[9]{0:T(128)S(1)} %get-tuple-element.69.steps, s32[9]{0:T(128)S(1)} %get-tuple-element.68.keys, bf16[64,1,2,64,128]{4,3,2,1,0:T(8,128)(2,1)S(1)} %copy-done.1, ...), custom_call_target="tpu_custom_call" | custom-call | flops 1000000000 | bytes 1000000 | tf_op jit(solution)/shard_map/pallas_call | solution.py:260
  87.8 3.7 %collective-permute-start.16 = (bf16[3,144,512]{2,1,0:T(8,128)(2,1)}, bf16[3,144,512]{2,1,0:T(8,128)(2,1)S(1)}, u32[]{:S(2)}, u32[]{:S(2)}) collective-permute-start(bf16[3,144,512]{2,1,0:T(8,128)(2,1)} %get-tuple-element.59), channel_id=1, source_target_pairs={{0,32},{1,9},{2,34},{3,11},{4,36},{5,13},{6,38},{7,15},{8,40},{9,1... | collective-permute-start | bytes 1327112 | tf_op jit(solution)/shard_map/ppermute | solution.py:313
  91.4 1.4 %collective-permute-start.17 = (bf16[3,144,512]{2,1,0:T(8,128)(2,1)}, bf16[3,144,512]{2,1,0:T(8,128)(2,1)S(1)}, u32[]{:S(2)}, u32[]{:S(2)}) collective-permute-start(bf16[3,144,512]{2,1,0:T(8,128)(2,1)} %get-tuple-element.60), channel_id=1, source_target_pairs={{0,96},{1,25},{2,98},{3,27},{4,100},{5,29},{6,102},{7,31},{8,104},... | collective-permute-start | bytes 1327112 | tf_op jit(solution)/shard_map/ppermute | solution.py:313
  92.8 1.1 %collective-permute-start.18 = (bf16[3,144,512]{2,1,0:T(8,128)(2,1)}, bf16[3,144,512]{2,1,0:T(8,128)(2,1)S(1)}, u32[]{:S(2)}, u32[]{:S(2)}) collective-permute-start(bf16[3,144,512]{2,1,0:T(8,128)(2,1)} %get-tuple-element.61), channel_id=1, source_target_pairs={{0,64},{1,17},{2,66},{3,19},{4,68},{5,21},{6,70},{7,23},{8,72},{9,... | collective-permute-start | bytes 1327112 | tf_op jit(solution)/shard_map/ppermute | solution.py:313
  93.9 0.1 slice.101.keys
  94.0 0.1 slice.100.steps
  94.1 0.7 reshape.276
  94.7 1.0 copy-done.5
  95.7 10.6 %shard_map.96 = (f32[3,128,512]{2,1,0:T(8,128)S(1)}, f32[3,8,512]{2,1,0:T(8,128)S(1)}) custom-call(s32[3,128]{1,0:T(4,128)S(1)} %slice.115.idx, s32[3]{0:T(128)S(1)} %slice.100.steps, s32[3]{0:T(128)S(1)} %slice.101.keys, bf16[64,1,2,64,128]{4,3,2,1,0:T(8,128)(2,1)} %refs_0_.5, bf16[64,1,2,64,128]{4,3,2,1,0:T(8,128)(2,1)} %copy-done, ...), custom_call_target="tpu_custom_call" | custom-call | flops 1000000000 | bytes 1000000 | tf_op jit(solution)/shard_map/pallas_call | solution.py:260
  106.3 0.0 collective-permute-done.16.a_ref
  106.3 1.2 %shard_map.98 = bf16[192,1024]{1,0:T(8,128)(2,1)} custom-call(f32[3,128,512]{2,1,0:T(8,128)S(1)} %get-tuple-element.54.o_ref, f32[3,8,512]{2,1,0:T(8,128)S(1)} %get-tuple-element.55.l_ref, bf16[3,144,512]{2,1,0:T(8,128)(2,1)S(1)} %collective-permute-done.16.a_ref, bf16[3,144,512]{2,1,0:T(8,128)(2,1)S(1)} %collective-permute-done.17.b_ref, ...), custom_call_target="tpu_custom_call" | custom-call | tf_op jit(solution)/shard_map/pallas_call | solution.py:358
  (39 shorter events, 0.2 us)
Async XLA Ops:
  0.6 15.6 %collective-permute-start.3 = (bf16[192,1024]{1,0:T(8,128)(2,1)}, bf16[192,1024]{1,0:T(8,128)(2,1)S(1)}, u32[]{:S(2)}, u32[]{:S(2)}) collective-permute-start(bf16[192,1024]{1,0:T(8,128)(2,1)} %refs_0_.3), channel_id=1, source_target_pairs={{0,2},{1,3},{2,4},{3,5},{4,6},{5,7},{6,0},{7,1},{8,10},{9,11},{10,... | collective-permute-start | bytes 1179656 | tf_op jit(solution)/shard_map/ppermute | solution.py:313
  3.2 13.1 %collective-permute-start.4 = (bf16[192,1024]{1,0:T(8,128)(2,1)}, bf16[192,1024]{1,0:T(8,128)(2,1)S(1)}, u32[]{:S(2)}, u32[]{:S(2)}) collective-permute-start(bf16[192,1024]{1,0:T(8,128)(2,1)} %refs_0_.3), channel_id=1, source_target_pairs={{0,6},{1,7},{2,0},{3,1},{4,2},{5,3},{6,4},{7,5},{8,14},{9,15},{10,... | collective-permute-start | bytes 1179656 | tf_op jit(solution)/shard_map/ppermute | solution.py:313
  5.4 18.3 %collective-permute-start.2 = (bf16[192,1024]{1,0:T(8,128)(2,1)}, bf16[192,1024]{1,0:T(8,128)(2,1)}, u32[]{:S(2)}, u32[]{:S(2)}) collective-permute-start(bf16[192,1024]{1,0:T(8,128)(2,1)} %refs_0_.3), channel_id=1, source_target_pairs={{0,1},{1,0},{2,3},{3,2},{4,5},{5,4},{6,7},{7,6},{8,9},{9,8},{10,11... | collective-permute-start | bytes 1179656 | tf_op jit(solution)/shard_map/ppermute | solution.py:313
  6.3 37.6 %collective-permute-start = (bf16[64,1,2,64,128]{4,3,2,1,0:T(8,128)(2,1)}, bf16[64,1,2,64,128]{4,3,2,1,0:T(8,128)(2,1)S(1)}, u32[]{:S(2)}, u32[]{:S(2)}) collective-permute-start(bf16[64,1,2,64,128]{4,3,2,1,0:T(8,128)(2,1)} %refs_0_.5), channel_id=1, source_target_pairs={{0,8},{1,33},{2,10},{3,35},{4,12},{5,37},{6,14},{7,39},{8,16},{9,4... | collective-permute-start | bytes 6291464 | tf_op jit(solution)/shard_map/ppermute | solution.py:313
  7.5 36.4 %collective-permute-start.1 = (bf16[64,1,2,64,128]{4,3,2,1,0:T(8,128)(2,1)}, bf16[64,1,2,64,128]{4,3,2,1,0:T(8,128)(2,1)}, u32[]{:S(2)}, u32[]{:S(2)}) collective-permute-start(bf16[64,1,2,64,128]{4,3,2,1,0:T(8,128)(2,1)} %refs_0_.5), channel_id=1, source_target_pairs={{0,24},{1,97},{2,26},{3,99},{4,28},{5,101},{6,30},{7,103},{8,0},{9... | collective-permute-start | bytes 6291464 | tf_op jit(solution)/shard_map/ppermute | solution.py:313
  16.3 6.1 %collective-permute-start.8 = (bf16[96,1024]{1,0:T(8,128)(2,1)S(1)}, bf16[96,1024]{1,0:T(8,128)(2,1)S(1)}, u32[]{:S(2)}, u32[]{:S(2)}) collective-permute-start(bf16[96,1024]{1,0:T(8,128)(2,1)S(1)} %slice.105), channel_id=1, source_target_pairs={{0,6},{1,7},{2,0},{3,1},{4,2},{5,3},{6,4},{7,5},{8,14},{9,15},{10,... | collective-permute-start | bytes 589832 | tf_op jit(solution)/shard_map/ppermute | solution.py:313
  18.1 7.0 %collective-permute-start.7 = (bf16[96,1024]{1,0:T(8,128)(2,1)S(1)}, bf16[96,1024]{1,0:T(8,128)(2,1)}, u32[]{:S(2)}, u32[]{:S(2)}) collective-permute-start(bf16[96,1024]{1,0:T(8,128)(2,1)S(1)} %slice.104), channel_id=1, source_target_pairs={{0,2},{1,3},{2,4},{3,5},{4,6},{5,7},{6,0},{7,1},{8,10},{9,11},{10,... | collective-permute-start | bytes 589832 | tf_op jit(solution)/shard_map/ppermute | solution.py:313
  22.4 4.4 %collective-permute-start.10 = (bf16[96,1024]{1,0:T(8,128)(2,1)S(1)}, bf16[96,1024]{1,0:T(8,128)(2,1)S(1)}, u32[]{:S(2)}, u32[]{:S(2)}) collective-permute-start(bf16[96,1024]{1,0:T(8,128)(2,1)S(1)} %collective-permute-done.8.refs_7_), channel_id=1, source_target_pairs={{0,1},{1,0},{2,3},{3,2},{4,5},{5,4},{6,7},{7,6},{8,9},{9,8},{10,11... | collective-permute-start | bytes 589832 | tf_op jit(solution)/shard_map/ppermute | solution.py:313
  23.7 5.5 %collective-permute-start.5 = (bf16[192,1024]{1,0:T(8,128)(2,1)S(1)}, bf16[192,1024]{1,0:T(8,128)(2,1)}, u32[]{:S(2)}, u32[]{:S(2)}) collective-permute-start(bf16[192,1024]{1,0:T(8,128)(2,1)S(1)} %collective-permute-done.3.refs_2_), channel_id=1, source_target_pairs={{0,1},{1,0},{2,3},{3,2},{4,5},{5,4},{6,7},{7,6},{8,9},{9,8},{10,11... | collective-permute-start | bytes 1179656 | tf_op jit(solution)/shard_map/ppermute | solution.py:313
  25.0 4.2 %collective-permute-start.6 = (bf16[192,1024]{1,0:T(8,128)(2,1)S(1)}, bf16[192,1024]{1,0:T(8,128)(2,1)}, u32[]{:S(2)}, u32[]{:S(2)}) collective-permute-start(bf16[192,1024]{1,0:T(8,128)(2,1)S(1)} %collective-permute-done.4.refs_3_), channel_id=1, source_target_pairs={{0,1},{1,0},{2,3},{3,2},{4,5},{5,4},{6,7},{7,6},{8,9},{9,8},{10,11... | collective-permute-start | bytes 1179656 | tf_op jit(solution)/shard_map/ppermute | solution.py:313
  26.8 0.7 copy-start.7
  27.4 1.8 %collective-permute-start.9 = (bf16[96,1024]{1,0:T(8,128)(2,1)}, bf16[96,1024]{1,0:T(8,128)(2,1)}, u32[]{:S(2)}, u32[]{:S(2)}) collective-permute-start(bf16[96,1024]{1,0:T(8,128)(2,1)} %collective-permute-done.7.refs_6_), channel_id=1, source_target_pairs={{0,1},{1,0},{2,3},{3,2},{4,5},{5,4},{6,7},{7,6},{8,9},{9,8},{10,11... | collective-permute-start | bytes 589832 | tf_op jit(solution)/shard_map/ppermute | solution.py:313
  29.2 1.0 copy-start.6
  30.2 0.9 copy-start.8
  43.9 2.9 %copy-start.4 = (bf16[3,128,512]{2,1,0:T(8,128)(2,1)}, bf16[3,128,512]{2,1,0:T(8,128)(2,1)S(1)}, u32[]{:S(2)}) copy-start(bf16[3,128,512]{2,1,0:T(8,128)(2,1)S(1)} %get-tuple-element.52.refs_5_) | copy-start | bytes 1179652
  43.9 26.9 %copy-start = (bf16[64,1,2,64,128]{4,3,2,1,0:T(8,128)(2,1)}, bf16[64,1,2,64,128]{4,3,2,1,0:T(8,128)(2,1)S(1)}, u32[]{:S(2)}) copy-start(bf16[64,1,2,64,128]{4,3,2,1,0:T(8,128)(2,1)S(1)} %collective-permute-done.refs_1_) | copy-start | bytes 6291460
  44.0 26.9 %copy-start.1 = (bf16[64,1,2,64,128]{4,3,2,1,0:T(8,128)(2,1)S(1)}, bf16[64,1,2,64,128]{4,3,2,1,0:T(8,128)(2,1)}, u32[]{:S(2)}) copy-start(bf16[64,1,2,64,128]{4,3,2,1,0:T(8,128)(2,1)} %refs_0_.5) | copy-start | bytes 6291460
  44.1 26.8 %collective-permute-start.11 = (bf16[32,1,2,64,128]{4,3,2,1,0:T(8,128)(2,1)S(1)}, bf16[32,1,2,64,128]{4,3,2,1,0:T(8,128)(2,1)S(1)}, u32[]{:S(2)}, u32[]{:S(2)}) collective-permute-start(bf16[32,1,2,64,128]{4,3,2,1,0:T(8,128)(2,1)S(1)} %slice.106), channel_id=1, source_target_pairs={{0,8},{1,33},{2,10},{3,35},{4,12},{5,37},{6,14},{7,39},{8,16},{9,4... | collective-permute-start | bytes 3145736 | tf_op jit(solution)/shard_map/ppermute | solution.py:313
  46.8 24.0 %collective-permute-start.12 = (bf16[32,1,2,64,128]{4,3,2,1,0:T(8,128)(2,1)S(1)}, bf16[32,1,2,64,128]{4,3,2,1,0:T(8,128)(2,1)S(1)}, u32[]{:S(2)}, u32[]{:S(2)}) collective-permute-start(bf16[32,1,2,64,128]{4,3,2,1,0:T(8,128)(2,1)S(1)} %slice.107), channel_id=1, source_target_pairs={{0,24},{1,97},{2,26},{3,99},{4,28},{5,101},{6,30},{7,103},{8,0},{9... | collective-permute-start | bytes 3145736 | tf_op jit(solution)/shard_map/ppermute | solution.py:313
  48.6 13.4 %collective-permute-start.13 = (bf16[3,144,512]{2,1,0:T(8,128)(2,1)S(1)}, bf16[3,144,512]{2,1,0:T(8,128)(2,1)S(1)}, u32[]{:S(2)}, u32[]{:S(2)}) collective-permute-start(bf16[3,144,512]{2,1,0:T(8,128)(2,1)S(1)} %get-tuple-element.56), channel_id=1, source_target_pairs={{0,96},{1,25},{2,98},{3,27},{4,100},{5,29},{6,102},{7,31},{8,104},... | collective-permute-start | bytes 1327112 | tf_op jit(solution)/shard_map/ppermute | solution.py:313
  51.1 14.5 %collective-permute-start.14 = (bf16[3,144,512]{2,1,0:T(8,128)(2,1)S(1)}, bf16[3,144,512]{2,1,0:T(8,128)(2,1)S(1)}, u32[]{:S(2)}, u32[]{:S(2)}) collective-permute-start(bf16[3,144,512]{2,1,0:T(8,128)(2,1)S(1)} %get-tuple-element.57), channel_id=1, source_target_pairs={{0,32},{1,9},{2,34},{3,11},{4,36},{5,13},{6,38},{7,15},{8,40},{9,1... | collective-permute-start | bytes 1327112 | tf_op jit(solution)/shard_map/ppermute | solution.py:313
  51.1 19.2 %collective-permute-start.15 = (bf16[3,144,512]{2,1,0:T(8,128)(2,1)S(1)}, bf16[3,144,512]{2,1,0:T(8,128)(2,1)S(1)}, u32[]{:S(2)}, u32[]{:S(2)}) collective-permute-start(bf16[3,144,512]{2,1,0:T(8,128)(2,1)S(1)} %get-tuple-element.58), channel_id=1, source_target_pairs={{0,64},{1,17},{2,66},{3,19},{4,68},{5,21},{6,70},{7,23},{8,72},{9,... | collective-permute-start | bytes 1327112 | tf_op jit(solution)/shard_map/ppermute | solution.py:313
  70.8 16.9 %copy-start.2 = (bf16[32,1,2,64,128]{4,3,2,1,0:T(8,128)(2,1)}, bf16[32,1,2,64,128]{4,3,2,1,0:T(8,128)(2,1)S(1)}, u32[]{:S(2)}) copy-start(bf16[32,1,2,64,128]{4,3,2,1,0:T(8,128)(2,1)S(1)} %collective-permute-done.11.refs_3_) | copy-start | bytes 3145732
  70.9 16.9 %copy-start.3 = (bf16[32,1,2,64,128]{4,3,2,1,0:T(8,128)(2,1)}, bf16[32,1,2,64,128]{4,3,2,1,0:T(8,128)(2,1)S(1)}, u32[]{:S(2)}) copy-start(bf16[32,1,2,64,128]{4,3,2,1,0:T(8,128)(2,1)S(1)} %collective-permute-done.12.refs_4_) | copy-start | bytes 3145732
  87.8 18.5 %collective-permute-start.16 = (bf16[3,144,512]{2,1,0:T(8,128)(2,1)}, bf16[3,144,512]{2,1,0:T(8,128)(2,1)S(1)}, u32[]{:S(2)}, u32[]{:S(2)}) collective-permute-start(bf16[3,144,512]{2,1,0:T(8,128)(2,1)} %get-tuple-element.59), channel_id=1, source_target_pairs={{0,32},{1,9},{2,34},{3,11},{4,36},{5,13},{6,38},{7,15},{8,40},{9,1... | collective-permute-start | bytes 1327112 | tf_op jit(solution)/shard_map/ppermute | solution.py:313
  91.4 14.9 %collective-permute-start.17 = (bf16[3,144,512]{2,1,0:T(8,128)(2,1)}, bf16[3,144,512]{2,1,0:T(8,128)(2,1)S(1)}, u32[]{:S(2)}, u32[]{:S(2)}) collective-permute-start(bf16[3,144,512]{2,1,0:T(8,128)(2,1)} %get-tuple-element.60), channel_id=1, source_target_pairs={{0,96},{1,25},{2,98},{3,27},{4,100},{5,29},{6,102},{7,31},{8,104},... | collective-permute-start | bytes 1327112 | tf_op jit(solution)/shard_map/ppermute | solution.py:313
  92.8 13.5 %collective-permute-start.18 = (bf16[3,144,512]{2,1,0:T(8,128)(2,1)}, bf16[3,144,512]{2,1,0:T(8,128)(2,1)S(1)}, u32[]{:S(2)}, u32[]{:S(2)}) collective-permute-start(bf16[3,144,512]{2,1,0:T(8,128)(2,1)} %get-tuple-element.61), channel_id=1, source_target_pairs={{0,64},{1,17},{2,66},{3,19},{4,68},{5,21},{6,70},{7,23},{8,72},{9,... | collective-permute-start | bytes 1327112 | tf_op jit(solution)/shard_map/ppermute | solution.py:313
  94.7 1.0 copy-start.5

commit v3 on v2

--- a/solution.py
+++ b/solution.py
@@ -127,14 +127,15 @@
     )(jnp.stack(ranks).astype(jnp.int32), *xs, wq, wk, wv, *rope, tails)
 
 
-def attend_kernel(groups, plan, idx, steps, keys, *refs):
+def attend_kernel(groups, plan, part, idx, steps, keys, *refs):
     refs = list(refs)
     take = lambda n: [refs.pop(0) for _ in range(n)]
     pages = take(len(plan))
     qs = take(len(groups))
     own = groups == (3,)
     suffix = take(1)[0] if own else None
-    outs = [take(2 if own else 1) for _ in groups]
+    before = take(3) if part == "far" else None
+    outs = [take(2)] if own else [take(3)] if part == "near" else [take(1) for _ in groups]
     pool, q_s, s_a, s_b, acc_s, sems = refs
 
     copies = []
@@ -180,6 +181,18 @@
     def finish(n, peak, total):
         total = jnp.sum(total, axis=0, keepdims=True)
         out = acc_s[...]
+        if part == "near":
+            outs[0][0][n] = out
+            outs[0][1][n] = jnp.broadcast_to(peak, (8, ROWS))
+            outs[0][2][n] = jnp.broadcast_to(total, (8, ROWS))
+            return
+        if part == "far":
+            old, old_total = before[1][n, :1], before[2][n, :1]
+            both = jnp.maximum(old, peak)
+            keep, new = jnp.exp2((old - both) * FACTOR), jnp.exp2((peak - both) * FACTOR)
+            out = out * new + before[0][n] * keep
+            total = total * new + old_total * keep
+            peak = both
         if own:
             r = pl.ds(pl.multiple_of(n * SUF, SUF), SUF)
             s = jnp.dot(suffix[r, :HD], q_s[n], preferred_element_type=jnp.float32)
@@ -245,20 +258,22 @@
     )
 
 
-def attend(groups, lists, pages, qs, suffix):
+def attend(groups, lists, pages, qs, suffix, part=None, before=()):
     own = groups == (3,)
     f32 = jnp.float32
     if own:
         outs = [jax.ShapeDtypeStruct((NODES, HD, ROWS), f32), jax.ShapeDtypeStruct((NODES, 8, ROWS), f32)]
+    elif part == "near":
+        outs = [jax.ShapeDtypeStruct((len(groups) * NODES, d, ROWS), f32) for d in (HD, 8, 8)]
     else:
         outs = [jax.ShapeDtypeStruct((NODES, HD + 16, ROWS), jnp.bfloat16) for _ in groups]
     n = len(groups) * NODES
-    extra = [suffix] if own else []
+    extra = ([suffix] if own else []) + list(before)
     vmem = pl.BlockSpec(memory_space=pltpu.VMEM)
     smem = pl.BlockSpec(memory_space=pltpu.SMEM)
     hbm = pl.BlockSpec(memory_space=pl.ANY)
     return pl.pallas_call(
-        functools.partial(attend_kernel, groups, tuple(at for at, _ in pages)),
+        functools.partial(attend_kernel, groups, tuple(at for at, _ in pages), part),
         out_shape=outs,
         in_specs=[smem] * 3 + [hbm] * len(pages) + [vmem] * (len(qs) + len(extra)),
         out_specs=[vmem] * len(outs),
@@ -328,11 +343,14 @@
     apart = (owner_page - along_page) % 4
     start = jnp.where(apart == 0, 0, jnp.where(apart == 3, 64, jnp.where(apart == 1, 128, 192)))
     valid = jnp.arange(MAXP, dtype=jnp.int32)[None, :] * PAGE < prefix_len[:, None]
-    masks = jnp.concatenate([valid & (owner_query == (along_query + d) % 4) for d in (1, -1, 2, 0)], axis=0)
-    idx, steps, keys = make_lists(masks, jnp.tile(start + page_slot, (4, 1)), jnp.tile(prefix_len, 4))
+    places = [valid & (owner_query == (along_query + d) % 4) for d in (1, -1, 2, 0)]
+    masks = [m & (apart != 2) for m in places[:3]] + [m & (apart == 2) for m in places[:3]] + places[3:]
+    where = [start + page_slot] * 3 + [page_slot] * 3 + [start + page_slot]
+    idx, steps, keys = make_lists(jnp.concatenate(masks, axis=0), jnp.concatenate(where, axis=0), jnp.tile(prefix_len, 7))
     numbers = jnp.stack([steps, keys // 64, keys % 64], axis=-1)
-    tails = jnp.zeros((9, 16, ROWS), jnp.bfloat16)
-    tails = tails.at[:, 0, :MAXP].set(idx[:9].astype(jnp.bfloat16)).at[:, 1, :3].set(numbers[:9].astype(jnp.bfloat16))
+    numbers = jnp.pad(numbers, ((0, 0), (0, MAXP - 3)))
+    tails = jnp.stack([idx[:9], numbers[:9], idx[9:18], numbers[9:18]], axis=1).astype(jnp.bfloat16)
+    tails = jnp.pad(tails, ((0, 0), (0, 12), (0, ROWS - MAXP)))
     tails = tails.reshape(3, NODES, 16, ROWS)
 
     tok_a, tok_b, tails, rope = lax.optimization_barrier((tok_a, tok_b, tails, rope))
@@ -346,15 +364,17 @@
     *sends, queries, suffix = project(blocks, ranks, w_query, w_key, w_value, rope, tails)
     suffix_kv = suffix.reshape(192, 2, 1, HD)
 
-    page_a, page_b, suffix = lax.optimization_barrier((page_a, page_b, suffix))
-    page_c, page_d = move(page_a[:32], page_shift(1)), move(page_b[32:], page_shift(-1))
     qs = [move(sends[1], query_shift(-1)), move(sends[0], query_shift(1)), move(sends[2], query_shift(2))]
-    got = jnp.concatenate([q[:, HD : HD + 2, :MAXP] for q in qs], axis=0).astype(jnp.int32)
-    theirs = (got[:, 0], got[:, 1, 0], got[:, 1, 1] * 64 + got[:, 1, 2])
+    page_al, page_bh, *qs = lax.optimization_barrier((page_a[:32], page_b[32:], *qs))
+    page_c, page_d = move(page_al, page_shift(1)), move(page_bh, page_shift(-1))
+    got = jnp.concatenate([q[:, HD : HD + 4, :MAXP] for q in qs], axis=0).astype(jnp.int32)
+    near, far = ((got[:, i], got[:, i + 1, 0], got[:, i + 1, 1] * 64 + got[:, i + 1, 2]) for i in (0, 2))
     pages = ((0, kv_pool), (64, page_a), (128, page_b), (192, page_c), (224, page_d))
-    sent = attend((0, 1, 2), theirs, pages, qs, None)
+    others = (0, 1, 2)
+    before = attend(others, near, pages[:3], qs, None, "near")
+    sent = attend(others, far, ((0, page_c), (32, page_d)), qs, None, "far", before)
     back = [move(r, query_shift(s)) for r, s in zip(sent, (1, -1, 2))]
-    mine = attend((3,), (idx[9:], steps[9:], keys[9:]), pages, [queries], suffix)
+    mine = attend((3,), (idx[18:], steps[18:], keys[18:]), pages, [queries], suffix)
     attended = pl.pallas_call(
         merge_kernel,
         out_shape=jax.ShapeDtypeStruct((192, 1024), jnp.bfloat16),

time: 109 us -> 109 us (level)
  the two profiles are of different devices: /device:TPU:1 before, /device:TPU:16 now
where the time goes in v3:
time: 109 us; the launch traced here: 107 us
  Pallas kernels  52.6 us (48%)
  starting transfers between devices  21 us (19%)
  waiting for transfers between devices  17.7 us (16%)
  local copies, waits for them, and re-layouts  8.69 us (8%)
  other arithmetic  6.31 us (6%)
    pallas_call x3, Pallas kernels, attend(): pl.pallas_call(functools.partial(attend_kernel, groups, tuple((at for at,...  38.2 us
    ppermute x19, starting transfers between devices, body(): move = lambda a, perm: lax.ppermute(a, AX, perm)  21 us
    ppermute x19, waiting for transfers between devices, body(): move = lambda a, perm: lax.ppermute(a, AX, perm)  17.7 us
    pallas_call x1, Pallas kernels, project(): pl.pallas_call(functools.partial(project_kernel, shape), out_shape=outs,...  13.2 us
    unnamed x25, local copies, waits for them, and re-layouts  2.79 us
  transfers between devices with their start and end apart: 19, of which 7 were waited for; matrix products, arithmetic and copies ran while one was open for 11% of the time, Pallas kernels for 38%

profile of v3, /device:TPU:16, one launch (start us, length us, event | category | flops | bytes accessed | tf_op | source)
XLA Modules:
  0.0 107.3 jit_solution(2693441408295713040)
XLA Ops:
  0.6 1.4 %collective-permute-start = (bf16[64,1,2,64,128]{4,3,2,1,0:T(8,128)(2,1)}, bf16[64,1,2,64,128]{4,3,2,1,0:T(8,128)(2,1)S(1)}, u32[]{:S(2)}, u32[]{:S(2)}) collective-permute-start(bf16[64,1,2,64,128]{4,3,2,1,0:T(8,128)(2,1)} %refs_0_.5), channel_id=1, source_target_pairs={{0,8},{1,33},{2,10},{3,35},{4,12},{5,37},{6,14},{7,39},{8,16},{9,4... | collective-permute-start | bytes 6291464 | tf_op jit(solution)/shard_map/ppermute | solution.py:328
  2.0 0.7 collective-permute-start.1
  2.7 0.5 collective-permute-start.2
  3.2 1.9 %collective-permute-start.3 = (bf16[192,1024]{1,0:T(8,128)(2,1)}, bf16[192,1024]{1,0:T(8,128)(2,1)S(1)}, u32[]{:S(2)}, u32[]{:S(2)}) collective-permute-start(bf16[192,1024]{1,0:T(8,128)(2,1)} %refs_0_.3), channel_id=1, source_target_pairs={{0,2},{1,3},{2,4},{3,5},{4,6},{5,7},{6,0},{7,1},{8,10},{9,11},{10,... | collective-permute-start | bytes 1179656 | tf_op jit(solution)/shard_map/ppermute | solution.py:328
  5.1 2.1 %collective-permute-start.4 = (bf16[192,1024]{1,0:T(8,128)(2,1)}, bf16[192,1024]{1,0:T(8,128)(2,1)S(1)}, u32[]{:S(2)}, u32[]{:S(2)}) collective-permute-start(bf16[192,1024]{1,0:T(8,128)(2,1)} %refs_0_.3), channel_id=1, source_target_pairs={{0,6},{1,7},{2,0},{3,1},{4,2},{5,3},{6,4},{7,5},{8,14},{9,15},{10,... | collective-permute-start | bytes 1179656 | tf_op jit(solution)/shard_map/ppermute | solution.py:328
  7.3 0.7 add_convert_fusion
  8.0 0.8 compare_and_fusion
  8.8 0.8 fusion.9
  9.6 0.7 select_add_fusion
  10.3 1.7 %concatenate.16 = s32[21,128]{1,0:T(8,128)S(1)} concatenate(s32[3,128]{1,0:T(4,128)S(1)} %select_add_fusion, s32[3,128]{1,0:T(4,128)S(1)} %select_add_fusion, s32[3,128]{1,0:T(4,128)S(1)} %select_add_fusion, s32[3,128]{1,0:T(4,128)} %param.14, s32[3,128]{1,0:T(4,128)} %param.14, s32[3,128]{1,0:T(4,128)} %param.14, s32[3,128]{1,0:T(4,128)S(1)} %select_add_fusion), dimensions={0} | concatenate | bytes 21504 | tf_op jit(solution)/shard_map/concatenate | solution.py:349
  11.9 0.7 fusion.10
  12.7 0.3 concatenate.15
  12.9 0.4 convert_reduce_fusion
  13.4 0.7 tile.2
  14.0 0.1 sub.72
  14.1 0.2 select_reduce_fusion.1
  14.3 0.0 copy-start.9
  14.3 0.5 select_reduce_fusion
  14.9 0.1 copy.33
  15.0 0.1 convert_element_type.25
  15.1 0.4 fusion.1
  15.6 0.1 pad_maximum_fusion
  15.7 1.0 collective-permute-done.3.refs_2_
  16.8 0.0 collective-permute-done.4.refs_3_
  16.8 1.3 %collective-permute-start.7 = (bf16[96,1024]{1,0:T(8,128)(2,1)S(1)}, bf16[96,1024]{1,0:T(8,128)(2,1)S(1)}, u32[]{:S(2)}, u32[]{:S(2)}) collective-permute-start(bf16[96,1024]{1,0:T(8,128)(2,1)S(1)} %slice.79), channel_id=1, source_target_pairs={{0,2},{1,3},{2,4},{3,5},{4,6},{5,7},{6,0},{7,1},{8,10},{9,11},{10,... | collective-permute-start | bytes 589832 | tf_op jit(solution)/shard_map/ppermute | solution.py:328
  18.1 0.0 collective-permute-done.2.refs_1_
  18.1 2.0 %collective-permute-start.8 = (bf16[96,1024]{1,0:T(8,128)(2,1)S(1)}, bf16[96,1024]{1,0:T(8,128)(2,1)}, u32[]{:S(2)}, u32[]{:S(2)}) collective-permute-start(bf16[96,1024]{1,0:T(8,128)(2,1)S(1)} %slice.80), channel_id=1, source_target_pairs={{0,6},{1,7},{2,0},{3,1},{4,2},{5,3},{6,4},{7,5},{8,14},{9,15},{10,... | collective-permute-start | bytes 589832 | tf_op jit(solution)/shard_map/ppermute | solution.py:328
  20.2 4.2 %collective-permute-done.7.refs_6_ = bf16[96,1024]{1,0:T(8,128)(2,1)S(1)} collective-permute-done((bf16[96,1024]{1,0:T(8,128)(2,1)S(1)}, bf16[96,1024]{1,0:T(8,128)(2,1)S(1)}, u32[]{:S(2)}, u32[]{:S(2)}) %collective-permute-start.7) | collective-permute-done | bytes 196640 | tf_op jit(solution)/shard_map/ppermute | solution.py:328
  24.4 0.0 collective-permute-start.6
  24.4 1.3 %collective-permute-done.8.refs_7_ = bf16[96,1024]{1,0:T(8,128)(2,1)} collective-permute-done((bf16[96,1024]{1,0:T(8,128)(2,1)S(1)}, bf16[96,1024]{1,0:T(8,128)(2,1)}, u32[]{:S(2)}, u32[]{:S(2)}) %collective-permute-start.8) | collective-permute-done | bytes 196640 | tf_op jit(solution)/shard_map/ppermute | solution.py:328
  25.6 0.0 collective-permute-start.9
  25.6 0.0 collective-permute-done.5.refs_4_
  25.6 0.7 copy-done.7
  26.4 0.5 collective-permute-start.10
  26.9 0.1 stack.61.ranks
  27.0 0.0 collective-permute-done.6.refs_5_
  27.0 0.2 collective-permute-done.9.refs_8_
  27.2 1.1 %collective-permute-done.10.refs_9_ = bf16[96,1024]{1,0:T(8,128)(2,1)} collective-permute-done((bf16[96,1024]{1,0:T(8,128)(2,1)}, bf16[96,1024]{1,0:T(8,128)(2,1)}, u32[]{:S(2)}, u32[]{:S(2)}) %collective-permute-start.10) | collective-permute-done | bytes 196640 | tf_op jit(solution)/shard_map/ppermute | solution.py:328
  28.3 1.0 copy-done.6
  29.3 1.0 copy-done.8
  30.3 13.2 %shard_map.95 = (bf16[3,144,512]{2,1,0:T(8,128)(2,1)S(1)}, bf16[3,144,512]{2,1,0:T(8,128)(2,1)S(1)}, bf16[3,144,512]{2,1,0:T(8,128)(2,1)S(1)}, bf16[3,128,512]{2,1,0:T(8,128)(2,1)S(1)}, bf16[192,256]{1,0:T(8,128)(2,1)S(1)}) custom-call(s32[8]{0:T(128)S(1)} %stack.61.ranks, bf16[192,1024]{1,0:T(8,128)(2,1)S(1)} %copy-done.6, ...), custom_call_target="tpu_custom_call" | custom-call | flops 1000000 | bytes 1000000 | tf_op jit(solution)/shard_map/pallas_call | solution.py:115
  43.5 0.0 copy-start.4
  43.5 2.8 %collective-permute-start.11 = (bf16[3,144,512]{2,1,0:T(8,128)(2,1)S(1)}, bf16[3,144,512]{2,1,0:T(8,128)(2,1)S(1)}, u32[]{:S(2)}, u32[]{:S(2)}) collective-permute-start(bf16[3,144,512]{2,1,0:T(8,128)(2,1)S(1)} %get-tuple-element.30), channel_id=1, source_target_pairs={{0,96},{1,25},{2,98},{3,27},{4,100},{5,29},{6,102},{7,31},{8,104},... | collective-permute-start | bytes 1327112 | tf_op jit(solution)/shard_map/ppermute | solution.py:328
  46.3 0.0 collective-permute-start.12
  46.3 2.3 %collective-permute-start.13 = (bf16[3,144,512]{2,1,0:T(8,128)(2,1)S(1)}, bf16[3,144,512]{2,1,0:T(8,128)(2,1)S(1)}, u32[]{:S(2)}, u32[]{:S(2)}) collective-permute-start(bf16[3,144,512]{2,1,0:T(8,128)(2,1)S(1)} %get-tuple-element.32), channel_id=1, source_target_pairs={{0,64},{1,17},{2,66},{3,19},{4,68},{5,21},{6,70},{7,23},{8,72},{9,... | collective-permute-start | bytes 1327112 | tf_op jit(solution)/shard_map/ppermute | solution.py:328
  48.6 0.1 slice.93
  48.7 0.0 collective-permute-done.1.refs_2_
  48.7 2.0 %slice.94 = bf16[32,1,2,64,128]{4,3,2,1,0:T(8,128)(2,1)S(1)} slice(bf16[64,1,2,64,128]{4,3,2,1,0:T(8,128)(2,1)} %collective-permute-done.1.refs_2_), slice={[32:64], [0:1], [0:2], [0:64], [0:128]} | slice | bytes 2097152 | tf_op jit(solution)/shard_map/slice | solution.py:368
  50.7 6.2 %collective-permute-done.11.refs_3_.refs_2_ = bf16[3,144,512]{2,1,0:T(8,128)(2,1)S(1)} collective-permute-done((bf16[3,144,512]{2,1,0:T(8,128)(2,1)S(1)}, bf16[3,144,512]{2,1,0:T(8,128)(2,1)S(1)}, u32[]{:S(2)}, u32[]{:S(2)}) %collective-permute-start.11) | collective-permute-done | bytes 442400 | tf_op jit(solution)/shard_map/ppermute | solution.py:328
  56.9 3.7 %collective-permute-done.12.refs_4_.refs_3_ = bf16[3,144,512]{2,1,0:T(8,128)(2,1)S(1)} collective-permute-done((bf16[3,144,512]{2,1,0:T(8,128)(2,1)S(1)}, bf16[3,144,512]{2,1,0:T(8,128)(2,1)S(1)}, u32[]{:S(2)}, u32[]{:S(2)}) %collective-permute-start.12) | collective-permute-done | bytes 442400 | tf_op jit(solution)/shard_map/ppermute | solution.py:328
  60.6 1.3 %collective-permute-start.14 = (bf16[32,1,2,64,128]{4,3,2,1,0:T(8,128)(2,1)S(1)}, bf16[32,1,2,64,128]{4,3,2,1,0:T(8,128)(2,1)S(1)}, u32[]{:S(2)}, u32[]{:S(2)}) collective-permute-start(bf16[32,1,2,64,128]{4,3,2,1,0:T(8,128)(2,1)S(1)} %slice.93), channel_id=1, source_target_pairs={{0,8},{1,33},{2,10},{3,35},{4,12},{5,37},{6,14},{7,39},{8,16},{9,4... | collective-permute-start | bytes 3145736 | tf_op jit(solution)/shard_map/ppermute | solution.py:328
  61.9 0.7 collective-permute-start.15
  62.7 0.8 fusion.3
  63.5 15.4 %shard_map.97 = (f32[9,128,512]{2,1,0:T(8,128)S(1)}, f32[9,8,512]{2,1,0:T(8,128)S(1)}, f32[9,8,512]{2,1,0:T(8,128)S(1)}) custom-call(s32[9,128]{1,0:T(8,128)S(1)} %bitcast.79, s32[9]{0:T(128)S(1)} %get-tuple-element.57.steps, s32[9]{0:T(128)S(1)} %get-tuple-element.56.keys, bf16[64,1,2,64,128]{4,3,2,1,0:T(8,128)(2,1)S(1)} %copy-done.1, ...), custom_call_target="tpu_custom_call" | custom-call | flops 1000000000 | bytes 1000000 | tf_op jit(solution)/shard_map/pallas_call | solution.py:275
  79.0 0.0 copy-start.10
  79.0 0.0 copy-start.5
  79.0 10.3 %shard_map.98 = (bf16[3,144,512]{2,1,0:T(8,128)(2,1)}, bf16[3,144,512]{2,1,0:T(8,128)(2,1)}, bf16[3,144,512]{2,1,0:T(8,128)(2,1)}) custom-call(s32[9,128]{1,0:T(8,128)S(1)} %bitcast.78, s32[9]{0:T(128)S(1)} %get-tuple-element.59.steps, s32[9]{0:T(128)S(1)} %get-tuple-element.58.keys, ...), custom_call_target="tpu_custom_call" | custom-call | flops 1000000000 | bytes 1000000 | tf_op jit(solution)/shard_map/pallas_call | solution.py:275
  89.3 0.1 collective-permute-start.16
  89.4 3.2 %collective-permute-start.17 = (bf16[3,144,512]{2,1,0:T(8,128)(2,1)}, bf16[3,144,512]{2,1,0:T(8,128)(2,1)S(1)}, u32[]{:S(2)}, u32[]{:S(2)}) collective-permute-start(bf16[3,144,512]{2,1,0:T(8,128)(2,1)} %get-tuple-element.46), channel_id=1, source_target_pairs={{0,96},{1,25},{2,98},{3,27},{4,100},{5,29},{6,102},{7,31},{8,104},... | collective-permute-start | bytes 1327112 | tf_op jit(solution)/shard_map/ppermute | solution.py:328
  92.6 0.1 slice.72.keys
  92.7 0.1 slice.71.steps
  92.8 0.7 reshape.198
  93.5 12.5 %shard_map.96 = (f32[3,128,512]{2,1,0:T(8,128)S(1)}, f32[3,8,512]{2,1,0:T(8,128)S(1)}) custom-call(s32[3,128]{1,0:T(4,128)S(1)} %slice.92.idx, s32[3]{0:T(128)S(1)} %slice.71.steps, s32[3]{0:T(128)S(1)} %slice.72.keys, bf16[64,1,2,64,128]{4,3,2,1,0:T(8,128)(2,1)} %refs_0_.5, bf16[64,1,2,64,128]{4,3,2,1,0:T(8,128)(2,1)} %copy-done, ...), custom_call_target="tpu_custom_call" | custom-call | flops 1000000000 | bytes 1000000 | tf_op jit(solution)/shard_map/pallas_call | solution.py:275
  106.0 1.2 %shard_map.99 = bf16[192,1024]{1,0:T(8,128)(2,1)} custom-call(f32[3,128,512]{2,1,0:T(8,128)S(1)} %get-tuple-element.37.o_ref, f32[3,8,512]{2,1,0:T(8,128)S(1)} %get-tuple-element.38.l_ref, bf16[3,144,512]{2,1,0:T(8,128)(2,1)S(1)} %collective-permute-done.16.a_ref, bf16[3,144,512]{2,1,0:T(8,128)(2,1)S(1)} %collective-permute-done.17.b_ref, ...), custom_call_target="tpu_custom_call" | custom-call | tf_op jit(solution)/shard_map/pallas_call | solution.py:378
  (50 shorter events, 0.3 us)
Async XLA Ops:
  0.6 48.0 %collective-permute-start = (bf16[64,1,2,64,128]{4,3,2,1,0:T(8,128)(2,1)}, bf16[64,1,2,64,128]{4,3,2,1,0:T(8,128)(2,1)S(1)}, u32[]{:S(2)}, u32[]{:S(2)}) collective-permute-start(bf16[64,1,2,64,128]{4,3,2,1,0:T(8,128)(2,1)} %refs_0_.5), channel_id=1, source_target_pairs={{0,8},{1,33},{2,10},{3,35},{4,12},{5,37},{6,14},{7,39},{8,16},{9,4... | collective-permute-start | bytes 6291464 | tf_op jit(solution)/shard_map/ppermute | solution.py:328
  2.0 46.7 %collective-permute-start.1 = (bf16[64,1,2,64,128]{4,3,2,1,0:T(8,128)(2,1)}, bf16[64,1,2,64,128]{4,3,2,1,0:T(8,128)(2,1)}, u32[]{:S(2)}, u32[]{:S(2)}) collective-permute-start(bf16[64,1,2,64,128]{4,3,2,1,0:T(8,128)(2,1)} %refs_0_.5), channel_id=1, source_target_pairs={{0,24},{1,97},{2,26},{3,99},{4,28},{5,101},{6,30},{7,103},{8,0},{9... | collective-permute-start | bytes 6291464 | tf_op jit(solution)/shard_map/ppermute | solution.py:328
  2.7 15.4 %collective-permute-start.2 = (bf16[192,1024]{1,0:T(8,128)(2,1)}, bf16[192,1024]{1,0:T(8,128)(2,1)}, u32[]{:S(2)}, u32[]{:S(2)}) collective-permute-start(bf16[192,1024]{1,0:T(8,128)(2,1)} %refs_0_.3), channel_id=1, source_target_pairs={{0,1},{1,0},{2,3},{3,2},{4,5},{5,4},{6,7},{7,6},{8,9},{9,8},{10,11... | collective-permute-start | bytes 1179656 | tf_op jit(solution)/shard_map/ppermute | solution.py:328
  3.2 13.5 %collective-permute-start.3 = (bf16[192,1024]{1,0:T(8,128)(2,1)}, bf16[192,1024]{1,0:T(8,128)(2,1)S(1)}, u32[]{:S(2)}, u32[]{:S(2)}) collective-permute-start(bf16[192,1024]{1,0:T(8,128)(2,1)} %refs_0_.3), channel_id=1, source_target_pairs={{0,2},{1,3},{2,4},{3,5},{4,6},{5,7},{6,0},{7,1},{8,10},{9,11},{10,... | collective-permute-start | bytes 1179656 | tf_op jit(solution)/shard_map/ppermute | solution.py:328
  5.1 11.6 %collective-permute-start.4 = (bf16[192,1024]{1,0:T(8,128)(2,1)}, bf16[192,1024]{1,0:T(8,128)(2,1)S(1)}, u32[]{:S(2)}, u32[]{:S(2)}) collective-permute-start(bf16[192,1024]{1,0:T(8,128)(2,1)} %refs_0_.3), channel_id=1, source_target_pairs={{0,6},{1,7},{2,0},{3,1},{4,2},{5,3},{6,4},{7,5},{8,14},{9,15},{10,... | collective-permute-start | bytes 1179656 | tf_op jit(solution)/shard_map/ppermute | solution.py:328
  14.3 0.6 copy-start.9
  16.8 7.6 %collective-permute-start.7 = (bf16[96,1024]{1,0:T(8,128)(2,1)S(1)}, bf16[96,1024]{1,0:T(8,128)(2,1)S(1)}, u32[]{:S(2)}, u32[]{:S(2)}) collective-permute-start(bf16[96,1024]{1,0:T(8,128)(2,1)S(1)} %slice.79), channel_id=1, source_target_pairs={{0,2},{1,3},{2,4},{3,5},{4,6},{5,7},{6,0},{7,1},{8,10},{9,11},{10,... | collective-permute-start | bytes 589832 | tf_op jit(solution)/shard_map/ppermute | solution.py:328
  18.1 7.5 %collective-permute-start.5 = (bf16[192,1024]{1,0:T(8,128)(2,1)S(1)}, bf16[192,1024]{1,0:T(8,128)(2,1)S(1)}, u32[]{:S(2)}, u32[]{:S(2)}) collective-permute-start(bf16[192,1024]{1,0:T(8,128)(2,1)S(1)} %collective-permute-done.3.refs_2_), channel_id=1, source_target_pairs={{0,1},{1,0},{2,3},{3,2},{4,5},{5,4},{6,7},{7,6},{8,9},{9,8},{10,11... | collective-permute-start | bytes 1179656 | tf_op jit(solution)/shard_map/ppermute | solution.py:328
  18.1 7.5 %collective-permute-start.8 = (bf16[96,1024]{1,0:T(8,128)(2,1)S(1)}, bf16[96,1024]{1,0:T(8,128)(2,1)}, u32[]{:S(2)}, u32[]{:S(2)}) collective-permute-start(bf16[96,1024]{1,0:T(8,128)(2,1)S(1)} %slice.80), channel_id=1, source_target_pairs={{0,6},{1,7},{2,0},{3,1},{4,2},{5,3},{6,4},{7,5},{8,14},{9,15},{10,... | collective-permute-start | bytes 589832 | tf_op jit(solution)/shard_map/ppermute | solution.py:328
  24.4 2.6 %collective-permute-start.6 = (bf16[192,1024]{1,0:T(8,128)(2,1)S(1)}, bf16[192,1024]{1,0:T(8,128)(2,1)}, u32[]{:S(2)}, u32[]{:S(2)}) collective-permute-start(bf16[192,1024]{1,0:T(8,128)(2,1)S(1)} %collective-permute-done.4.refs_3_), channel_id=1, source_target_pairs={{0,1},{1,0},{2,3},{3,2},{4,5},{5,4},{6,7},{7,6},{8,9},{9,8},{10,11... | collective-permute-start | bytes 1179656 | tf_op jit(solution)/shard_map/ppermute | solution.py:328
  25.6 1.6 %collective-permute-start.9 = (bf16[96,1024]{1,0:T(8,128)(2,1)S(1)}, bf16[96,1024]{1,0:T(8,128)(2,1)}, u32[]{:S(2)}, u32[]{:S(2)}) collective-permute-start(bf16[96,1024]{1,0:T(8,128)(2,1)S(1)} %collective-permute-done.7.refs_6_), channel_id=1, source_target_pairs={{0,1},{1,0},{2,3},{3,2},{4,5},{5,4},{6,7},{7,6},{8,9},{9,8},{10,11... | collective-permute-start | bytes 589832 | tf_op jit(solution)/shard_map/ppermute | solution.py:328
  25.6 0.7 copy-start.7
  26.4 1.9 %collective-permute-start.10 = (bf16[96,1024]{1,0:T(8,128)(2,1)}, bf16[96,1024]{1,0:T(8,128)(2,1)}, u32[]{:S(2)}, u32[]{:S(2)}) collective-permute-start(bf16[96,1024]{1,0:T(8,128)(2,1)} %collective-permute-done.8.refs_7_), channel_id=1, source_target_pairs={{0,1},{1,0},{2,3},{3,2},{4,5},{5,4},{6,7},{7,6},{8,9},{9,8},{10,11... | collective-permute-start | bytes 589832 | tf_op jit(solution)/shard_map/ppermute | solution.py:328
  28.3 1.0 copy-start.6
  29.3 1.0 copy-start.8
  43.5 7.2 %copy-start.4 = (bf16[3,128,512]{2,1,0:T(8,128)(2,1)}, bf16[3,128,512]{2,1,0:T(8,128)(2,1)S(1)}, u32[]{:S(2)}) copy-start(bf16[3,128,512]{2,1,0:T(8,128)(2,1)S(1)} %get-tuple-element.35.refs_5_) | copy-start | bytes 1179652
  43.5 13.4 %collective-permute-start.11 = (bf16[3,144,512]{2,1,0:T(8,128)(2,1)S(1)}, bf16[3,144,512]{2,1,0:T(8,128)(2,1)S(1)}, u32[]{:S(2)}, u32[]{:S(2)}) collective-permute-start(bf16[3,144,512]{2,1,0:T(8,128)(2,1)S(1)} %get-tuple-element.30), channel_id=1, source_target_pairs={{0,96},{1,25},{2,98},{3,27},{4,100},{5,29},{6,102},{7,31},{8,104},... | collective-permute-start | bytes 1327112 | tf_op jit(solution)/shard_map/ppermute | solution.py:328
  46.3 14.3 %collective-permute-start.12 = (bf16[3,144,512]{2,1,0:T(8,128)(2,1)S(1)}, bf16[3,144,512]{2,1,0:T(8,128)(2,1)S(1)}, u32[]{:S(2)}, u32[]{:S(2)}) collective-permute-start(bf16[3,144,512]{2,1,0:T(8,128)(2,1)S(1)} %get-tuple-element.31), channel_id=1, source_target_pairs={{0,32},{1,9},{2,34},{3,11},{4,36},{5,13},{6,38},{7,15},{8,40},{9,1... | collective-permute-start | bytes 1327112 | tf_op jit(solution)/shard_map/ppermute | solution.py:328
  46.3 17.2 %copy-start.1 = (bf16[64,1,2,64,128]{4,3,2,1,0:T(8,128)(2,1)S(1)}, bf16[64,1,2,64,128]{4,3,2,1,0:T(8,128)(2,1)}, u32[]{:S(2)}) copy-start(bf16[64,1,2,64,128]{4,3,2,1,0:T(8,128)(2,1)} %refs_0_.5) | copy-start | bytes 6291460
  46.3 14.3 %collective-permute-start.13 = (bf16[3,144,512]{2,1,0:T(8,128)(2,1)S(1)}, bf16[3,144,512]{2,1,0:T(8,128)(2,1)S(1)}, u32[]{:S(2)}, u32[]{:S(2)}) collective-permute-start(bf16[3,144,512]{2,1,0:T(8,128)(2,1)S(1)} %get-tuple-element.32), channel_id=1, source_target_pairs={{0,64},{1,17},{2,66},{3,19},{4,68},{5,21},{6,70},{7,23},{8,72},{9,... | collective-permute-start | bytes 1327112 | tf_op jit(solution)/shard_map/ppermute | solution.py:328
  48.6 14.9 %copy-start = (bf16[64,1,2,64,128]{4,3,2,1,0:T(8,128)(2,1)}, bf16[64,1,2,64,128]{4,3,2,1,0:T(8,128)(2,1)S(1)}, u32[]{:S(2)}) copy-start(bf16[64,1,2,64,128]{4,3,2,1,0:T(8,128)(2,1)S(1)} %collective-permute-done.refs_1_) | copy-start | bytes 6291460
  60.6 18.4 %collective-permute-start.14 = (bf16[32,1,2,64,128]{4,3,2,1,0:T(8,128)(2,1)S(1)}, bf16[32,1,2,64,128]{4,3,2,1,0:T(8,128)(2,1)S(1)}, u32[]{:S(2)}, u32[]{:S(2)}) collective-permute-start(bf16[32,1,2,64,128]{4,3,2,1,0:T(8,128)(2,1)S(1)} %slice.93), channel_id=1, source_target_pairs={{0,8},{1,33},{2,10},{3,35},{4,12},{5,37},{6,14},{7,39},{8,16},{9,4... | collective-permute-start | bytes 3145736 | tf_op jit(solution)/shard_map/ppermute | solution.py:328
  61.9 17.1 %collective-permute-start.15 = (bf16[32,1,2,64,128]{4,3,2,1,0:T(8,128)(2,1)S(1)}, bf16[32,1,2,64,128]{4,3,2,1,0:T(8,128)(2,1)S(1)}, u32[]{:S(2)}, u32[]{:S(2)}) collective-permute-start(bf16[32,1,2,64,128]{4,3,2,1,0:T(8,128)(2,1)S(1)} %slice.94), channel_id=1, source_target_pairs={{0,24},{1,97},{2,26},{3,99},{4,28},{5,101},{6,30},{7,103},{8,0},{9... | collective-permute-start | bytes 3145736 | tf_op jit(solution)/shard_map/ppermute | solution.py:328
  79.0 10.3 %copy-start.2 = (bf16[32,1,2,64,128]{4,3,2,1,0:T(8,128)(2,1)}, bf16[32,1,2,64,128]{4,3,2,1,0:T(8,128)(2,1)S(1)}, u32[]{:S(2)}) copy-start(bf16[32,1,2,64,128]{4,3,2,1,0:T(8,128)(2,1)S(1)} %collective-permute-done.14.refs_3_.refs_0_) | copy-start | bytes 3145732
  79.0 10.3 %copy-start.3 = (bf16[32,1,2,64,128]{4,3,2,1,0:T(8,128)(2,1)}, bf16[32,1,2,64,128]{4,3,2,1,0:T(8,128)(2,1)S(1)}, u32[]{:S(2)}) copy-start(bf16[32,1,2,64,128]{4,3,2,1,0:T(8,128)(2,1)S(1)} %collective-permute-done.15.refs_4_.refs_1_) | copy-start | bytes 3145732
  79.0 13.6 %copy-start.10 = (s32[21]{0:T(128)S(1)}, s32[21]{0:T(128)}, u32[]{:S(2)}) copy-start(s32[21]{0:T(128)} %copy-done.9) | copy-start | bytes 256
  79.0 14.5 %copy-start.5 = (bf16[3,128,512]{2,1,0:T(8,128)(2,1)S(1)}, bf16[3,128,512]{2,1,0:T(8,128)(2,1)}, u32[]{:S(2)}) copy-start(bf16[3,128,512]{2,1,0:T(8,128)(2,1)} %copy-done.4) | copy-start | bytes 1179652
  89.3 16.7 %collective-permute-start.16 = (bf16[3,144,512]{2,1,0:T(8,128)(2,1)}, bf16[3,144,512]{2,1,0:T(8,128)(2,1)S(1)}, u32[]{:S(2)}, u32[]{:S(2)}) collective-permute-start(bf16[3,144,512]{2,1,0:T(8,128)(2,1)} %get-tuple-element.45), channel_id=1, source_target_pairs={{0,32},{1,9},{2,34},{3,11},{4,36},{5,13},{6,38},{7,15},{8,40},{9,1... | collective-permute-start | bytes 1327112 | tf_op jit(solution)/shard_map/ppermute | solution.py:328
  89.4 16.6 %collective-permute-start.17 = (bf16[3,144,512]{2,1,0:T(8,128)(2,1)}, bf16[3,144,512]{2,1,0:T(8,128)(2,1)S(1)}, u32[]{:S(2)}, u32[]{:S(2)}) collective-permute-start(bf16[3,144,512]{2,1,0:T(8,128)(2,1)} %get-tuple-element.46), channel_id=1, source_target_pairs={{0,96},{1,25},{2,98},{3,27},{4,100},{5,29},{6,102},{7,31},{8,104},... | collective-permute-start | bytes 1327112 | tf_op jit(solution)/shard_map/ppermute | solution.py:328
  92.6 13.4 %collective-permute-start.18 = (bf16[3,144,512]{2,1,0:T(8,128)(2,1)}, bf16[3,144,512]{2,1,0:T(8,128)(2,1)S(1)}, u32[]{:S(2)}, u32[]{:S(2)}) collective-permute-start(bf16[3,144,512]{2,1,0:T(8,128)(2,1)} %get-tuple-element.47), channel_id=1, source_target_pairs={{0,64},{1,17},{2,66},{3,19},{4,68},{5,21},{6,70},{7,23},{8,72},{9,... | collective-permute-start | bytes 1327112 | tf_op jit(solution)/shard_map/ppermute | solution.py:328
